TPU v7x, 512 devices: a whole 4x4x16 slice. The times are simulated.
512 devices in a mesh: ka: 8 (over z_lo), atoms: 64 (over y, z_hi, x, core).
Axes of the slice: x: 4, y: 4, z: 16 (z_hi: 2, z_lo: 8; z = z_hi * 8 + z_lo), core: 2. Of those that a mesh axis runs over, the one named last changes fastest.
Arguments:
- positions: float32 [3, 262144], P(None, ('ka', 'atoms')), may hold values from 0 to 1
- charges: float32 [8, 262144], P(None, ('ka', 'atoms')), may hold values from -6 to 6
- miller: int32 [3, 4096], P(None, 'ka'), may hold values from -10 to 10, as said below
Outputs:
- energies: float32 [262144], P(('ka', 'atoms'))
- forces: float32 [3, 262144], P(None, ('ka', 'atoms'))
Inputs may be any that keep to these rules, and one draw needn't show every extreme that they name: `miller`: the columns are distinct nonzero triples.
All inputs are finite; a program needn't handle non-finite values.
Results may differ from a plain program's by a relative error of at most 0.0003.
Values sent between devices are 32-bit elements; how exact they have to be, the bound alone decides.
No kernel may reach another device: no remote copies, remote signals or barrier semaphores. Data moves between devices by JAX's collectives and lax.ppermute only.
A program may use at most 64 MiB of HBM per device.

v0:
```python
import jax
import jax.numpy as jnp
from jax import lax
from jax.sharding import PartitionSpec as P


def phase_tiles(miller_f, pos):
    angle = (
        2.0
        * jnp.pi
        * jnp.dot(
            miller_f.T, pos, precision=lax.Precision.HIGHEST, preferred_element_type=jnp.float32
        )
    )
    return (jnp.cos(angle), jnp.sin(angle))


def struct_from_tiles(cosines, sines, chg):
    real_part = jnp.dot(
        cosines, chg.T, precision=lax.Precision.HIGHEST, preferred_element_type=jnp.float32
    )
    imag_part = jnp.dot(
        sines, chg.T, precision=lax.Precision.HIGHEST, preferred_element_type=jnp.float32
    )
    return jnp.concatenate([real_part, imag_part], axis=1)


def partial_struct(miller_f, pos, chg):
    cosines, sines = phase_tiles(miller_f, pos)
    return struct_from_tiles(cosines, sines, chg)


def all_indices(miller):
    return lax.all_gather(miller, "ka", axis=1, tiled=True).astype(jnp.float32)


def apply_struct(struct, miller_f, cosines, sines, chg):
    latent = chg.shape[0]
    msq = jnp.sum(miller_f * miller_f, axis=0)
    weight = jnp.exp(-0.025 * msq) / msq
    real_w = weight[:, None] * struct[:, :latent]
    imag_w = weight[:, None] * struct[:, latent:]
    left_cos = jnp.concatenate(
        [real_w] + [-miller_f[d][:, None] * imag_w for d in range(3)], axis=1
    )
    left_sin = jnp.concatenate([imag_w] + [miller_f[d][:, None] * real_w for d in range(3)], axis=1)
    total = jnp.dot(
        left_cos.T, cosines, precision=lax.Precision.HIGHEST, preferred_element_type=jnp.float32
    )
    total = total + jnp.dot(
        left_sin.T, sines, precision=lax.Precision.HIGHEST, preferred_element_type=jnp.float32
    )
    energy = 0.25 * jnp.sum(chg * total[:latent], axis=0)
    force = jnp.stack(
        [0.1 * jnp.sum(chg * total[latent * (d + 1) : latent * (d + 2)], axis=0) for d in range(3)]
    )
    return jnp.concatenate([energy[None, :], force], axis=0)


def per_device(positions, charges, miller):
    total_atoms = positions.shape[1] * lax.axis_size("ka") * lax.axis_size("atoms")
    scale = jnp.sqrt(jnp.float32(total_atoms))
    own_f = miller.astype(jnp.float32)
    block_sum = partial_struct(
        own_f,
        lax.all_gather(positions, "ka", axis=1, tiled=True),
        lax.all_gather(charges, "ka", axis=1, tiled=True),
    )
    block_total = lax.psum(block_sum, "atoms")
    struct = lax.all_gather(block_total, "ka", axis=0, tiled=True)
    every_f = all_indices(miller)
    struct = struct / scale
    cosines, sines = phase_tiles(every_f, positions)
    result = apply_struct(struct, every_f, cosines, sines, charges)
    return (result[0], result[1:])


def solution(mesh):
    in_specs = (P(None, ("ka", "atoms")), P(None, ("ka", "atoms")), P(None, "ka"))
    out_specs = (P(("ka", "atoms")), P(None, ("ka", "atoms")))
    return jax.shard_map(
        per_device, mesh=mesh, in_specs=in_specs, out_specs=out_specs, check_vma=False
    )
```

profile of v0, /device:TPU:32, one launch (start us, length us, event | category | flops | bytes accessed | tf_op | source)
XLA Modules:
  0.0 899.3 jit_solution(8823628775523412769)
XLA Ops:
  0.6 49.1 %all_gather.12 = s32[3,4096]{1,0:T(4,128)S(1)} all-gather(s32[3,512]{1,0:T(4,128)} %param.5), channel_id=1, replica_groups=mesh['ka'=8,'atoms'=64] {'ka'}, dimensions={1}, use_global_device_ids=true | all-gather | bytes 55296 | tf_op jit(solution)/shard_map/all_gather | solution.py:34
  49.9 46.4 %all_gather.13 = f32[3,4096]{1,0:T(4,128)S(1)} all-gather(f32[3,512]{1,0:T(4,128)} %param.3), channel_id=1, replica_groups=mesh['ka'=8,'atoms'=64] {'ka'}, dimensions={1}, use_global_device_ids=true | all-gather | bytes 55296 | tf_op jit(solution)/shard_map/all_gather | solution.py:66
  96.4 46.5 %all_gather.14 = f32[8,4096]{1,0:T(8,128)S(1)} all-gather(f32[8,512]{1,0:T(8,128)} %param.4), channel_id=1, replica_groups=mesh['ka'=8,'atoms'=64] {'ka'}, dimensions={1}, use_global_device_ids=true | all-gather | bytes 147456 | tf_op jit(solution)/shard_map/all_gather | solution.py:67
  142.9 7.4 fusion.37
  150.3 0.0 copy-start.1
  150.3 38.3 %fusion.4 = f32[512,8]{0,1:T(8,128)S(1)} fusion(f32[8,4096]{1,0:T(8,128)S(1)} %all_gather.14, f32[512,4096]{1,0:T(8,128)S(1)} %fusion.37), kind=kOutput, calls=%fused_computation.4 | convolution fusion | flops 203423744 | bytes 8536064 | tf_op jit(solution)/shard_map/dot_general | solution.py:22
  188.6 38.0 %fusion.6 = f32[512,8]{0,1:T(8,128)S(1)} fusion(f32[8,4096]{1,0:T(8,128)S(1)} %all_gather.14, f32[512,4096]{1,0:T(8,128)S(1)} %fusion.37), kind=kOutput, calls=%fused_computation.6 | convolution fusion | flops 203423744 | bytes 8536064 | tf_op jit(solution)/shard_map/dot_general | solution.py:19
  226.6 553.9 %psum.7 = f32[512,16]{0,1:T(8,128)S(1)} all-reduce(f32[512,16]{0,1:T(8,128)S(1)} %pad_maximum_fusion), channel_id=1, replica_groups=mesh['ka'=8,'atoms'=64] {'atoms'}, use_global_device_ids=true, to_apply=%region_1.0 | all-reduce | flops 8192 | bytes 65536 | tf_op jit(solution)/shard_map/psum | solution.py:69
  780.5 46.8 %all_gather.15 = f32[4096,16]{0,1:T(8,128)S(1)} all-gather(f32[512,16]{0,1:T(8,128)S(1)} %psum.7), channel_id=1, replica_groups=mesh['ka'=8,'atoms'=64] {'ka'}, dimensions={0}, use_global_device_ids=true | all-gather | bytes 294912 | tf_op jit(solution)/shard_map/all_gather | solution.py:70
  827.4 0.1 broadcast_multiply_fusion.6
  827.4 0.1 broadcast_multiply_fusion.2
  827.5 0.0 copy-done.1
  827.5 6.7 fusion.45
  834.2 0.0 copy-start
  834.2 32.3 %fusion = f32[32,512]{1,0:T(8,128)S(1)} fusion(f32[4096,512]{1,0:T(8,128)S(1)} %fusion.45, f32[4096,8]{0,1:T(8,128)S(1)} %get-tuple-element.15, f32[4096,8]{0,1:T(8,128)S(1)} %get-tuple-element.14, f32[4096,8]{0,1:T(8,128)S(1)} %get-tuple-element.10, f32[4096,8]{0,1:T(8,128)S(1)} %get-tuple-element.7), kind=kOutput, calls=%fused_computation | convolution fusion | flops 807796736 | bytes 8978432 | tf_op jit(solution)/shard_map/dot_general | solution.py:50
  866.5 31.4 %fusion.16 = f32[32,512]{1,0:T(8,128)S(1)} fusion(f32[32,512]{1,0:T(8,128)S(1)} %fusion, f32[4096,512]{1,0:T(8,128)S(1)} %fusion.45, f32[4096,8]{0,1:T(8,128)S(1)} %get-tuple-element.19, f32[4096,8]{0,1:T(8,128)S(1)} %get-tuple-element.20, f32[4096,8]{0,1:T(8,128)S(1)} %get-tuple-element.6, f32[4096,8]{0,1:T(8,128)S(1)} %get-tuple-element.11), kind=kOutput, calls=%fused_computation.16 | convolution fusion | flops 807813120 | bytes 9043968 | tf_op jit(solution)/shard_map/dot_general | solution.py:47
  897.9 0.0 copy-done
  897.9 0.6 broadcast_multiply_fusion.10
  898.5 0.6 pad_maximum_fusion.1
  (13 shorter events, 0.2 us)
Async XLA Ops:
  150.3 677.1 %copy-start.1 = (f32[3,512]{1,0:T(4,128)S(1)}, f32[3,512]{1,0:T(4,128)}, u32[]{:S(2)}) copy-start(f32[3,512]{1,0:T(4,128)} %param.3) | copy-start | bytes 18436
  834.2 63.7 %copy-start = (f32[8,512]{1,0:T(8,128)S(1)}, f32[8,512]{1,0:T(8,128)}, u32[]{:S(2)}) copy-start(f32[8,512]{1,0:T(8,128)} %param.4) | copy-start | bytes 49156
where the time goes:
time: 907 us; the launch traced here: 899 us
  blocking collectives  743 us (82%)
  matrix products  154 us (17%)
    psum x1, blocking collectives, per_device(): block_total = lax.psum(block_sum, 'atoms')  554 us
    all_gather x1, blocking collectives, all_indices(): return lax.all_gather(miller, 'ka', axis=1, tiled=True).astype(jnp.float32)  49.1 us
    all_gather x1, blocking collectives, per_device(): struct = lax.all_gather(block_total, 'ka', axis=0, tiled=True)  46.8 us
    all_gather x1, blocking collectives, per_device(): lax.all_gather(charges, 'ka', axis=1, tiled=True)  46.5 us
    all_gather x1, blocking collectives, per_device(): lax.all_gather(positions, 'ka', axis=1, tiled=True)  46.4 us
    dot_general x1, matrix products, struct_from_tiles(): jnp.dot(sines, chg.T, precision=lax.Precision.HIGHEST, preferred_element_...  38.3 us
    dot_general x1, matrix products, struct_from_tiles(): jnp.dot(cosines, chg.T, precision=lax.Precision.HIGHEST, preferred_elemen...  38 us
    dot_general x1, matrix products, apply_struct(): jnp.dot(left_sin.T, sines, precision=lax.Precision.HIGHEST, preferred_ele...  32.3 us

commit v1 on v0

v1 whole, which is shorter than its diff:
```python
import functools

import jax
import jax.numpy as jnp
from jax import lax
from jax.experimental import pallas as pl
from jax.experimental.pallas import tpu as pltpu
from jax.sharding import Mesh
from jax.sharding import PartitionSpec as P

TOP = 10
LATENT = 8
TILES = 32
ROWS = 8
HALF = 176
LANES = 384
COUNT_LANE = 352
SIN = (3.141592640130706, -5.167710083507839, 2.550077523214083, -0.5982912856178239, 0.07765766030006041)
COS = (
    1.0,
    -4.934802137078852,
    4.058709159556494,
    -1.3352120030499017,
    0.23493731380758293,
    -0.02439632432974524,
)
F32 = jnp.float32
BF16 = jnp.bfloat16
SPREAD = ("y", "x", "c")
COLUMN = ("zl", "zh")


def horner(coefs, u):
    out = jnp.full_like(u, coefs[-1])
    for c in coefs[-2::-1]:
        out = out * u + c
    return out


def orders(shape):
    r = lax.broadcasted_iota(jnp.int32, shape, 0)
    late = jnp.where(r == 9, 9, jnp.where(r == 10, 10, jnp.where(r == 11, -9, jnp.where(r == 12, -10, 0))))
    return jnp.where(r < 8, r + 1, late).astype(F32)


def table(coordinate):
    t = orders((16, coordinate.shape[1])) * coordinate
    t = t - jnp.round(t)
    u = t * t
    s = t * horner(SIN, u)
    c = horner(COS, u)
    return 1.0 - 2.0 * s * s, 2.0 * s * c


def row_of(n):
    n = abs(n)
    return n - 1 if 1 <= n <= 8 else (8 if n == 0 else n)


def split(x):
    high = x.astype(BF16)
    return high, (x - high.astype(F32)).astype(BF16)


def pair_tile(tile, cx, sx, cy, sy):
    if tile < 21:
        b = tile - TOP
        r = row_of(b)
        ca, sa, cb, sb = cx[0:8], sx[0:8], cy[r : r + 1], sy[r : r + 1]
        minus = b < 0
    elif tile < 30:
        i, j = divmod(tile - 21, 3)
        r = 8 + i
        ca, sa = cx[r : r + 1], sx[r : r + 1]
        rows = slice(8, 16) if j == 2 else slice(0, 8)
        cb, sb = cy[rows], sy[rows]
        minus = j == 1
    else:
        zero = jnp.zeros((8, cx.shape[1]), F32)
        return zero, zero
    cc, ss, sc, cs = ca * cb, sa * sb, sa * cb, ca * sb
    if minus:
        return cc + ss, sc - cs
    return cc - ss, sc + cs


def z_rows(rows, charges):
    return [rows[row_of(n) : row_of(n) + 1] * charges for n in range(TOP + 1)]


def nt(a, b):
    return lax.dot_general(a, b, (((1,), (1,)), ((), ())), preferred_element_type=F32)


def nn(a, b):
    return jnp.dot(a, b, preferred_element_type=F32)


def product(mul, a, b):
    return mul(a[0], b[0]) + (mul(a[0], b[1]) + mul(a[1], b[0]))


def struct_kernel(pos_ref, chg_ref, out_ref, re_hi, re_lo, im_hi, im_lo):
    charges = chg_ref[...]
    atoms = charges.shape[1]
    cx, sx = table(pos_ref[0:1, :])
    cy, sy = table(pos_ref[1:2, :])
    cz, sz = table(pos_ref[2:3, :])
    for two in range(TILES // 2):
        first = pair_tile(2 * two, cx, sx, cy, sy)
        second = pair_tile(2 * two + 1, cx, sx, cy, sy)
        rows = slice(16 * two, 16 * two + 16)
        re_hi[rows, :], re_lo[rows, :] = split(jnp.concatenate([first[0], second[0]], axis=0))
        im_hi[rows, :], im_lo[rows, :] = split(jnp.concatenate([first[1], second[1]], axis=0))
    cq = z_rows(cz, charges)
    sq = z_rows(sz, charges)
    blank = lambda n: [jnp.zeros((n, atoms), F32)]
    real = product(nt, (re_hi[...], re_lo[...]), split(jnp.concatenate(cq + sq + blank(80), axis=0)))
    imag = product(nt, (im_hi[...], im_lo[...]), split(jnp.concatenate(blank(48) + sq + cq + blank(32), axis=0)))
    out_ref[:, :, 0:128] = real[:, 0:128].reshape(TILES, ROWS, 128)
    out_ref[:, :, 128:256] = (real[:, 128:256] + imag[:, 0:128]).reshape(TILES, ROWS, 128)
    out_ref[:, :, 256:384] = imag[:, 128:256].reshape(TILES, ROWS, 128)


def slot_of(a, b):
    ordinary = (a >= 1) & (a <= 8)
    i = jnp.where(a == 9, 1, jnp.where(a == 10, 2, 0))
    up = (b >= 1) & (b <= 8)
    down = (b <= -1) & (b >= -8)
    j = jnp.where(up, 0, jnp.where(down, 1, 2))
    rest = jnp.where(b == 9, 1, jnp.where(b == 10, 2, jnp.where(b == -9, 3, jnp.where(b == -10, 4, 0))))
    row = jnp.where(up, b - 1, jnp.where(down, -b - 1, rest))
    return jnp.where(ordinary, (b + TOP) * 8 + a - 1, (21 + i * 3 + j) * 8 + row)


def collect_kernel(tile_ref, part_ref, miller_ref, out_ref):
    total = jnp.sum(part_ref[...], axis=0)
    a, b, c = miller_ref[0:1, :], miller_ref[1:2, :], miller_ref[2:3, :]
    sign = jnp.where(a < 0, -1, 1)
    a, b, c = a * sign, b * sign, c * sign
    listed = a.shape[1]
    slot = slot_of(a, b) - tile_ref[0] * 8
    pair = (slot == lax.broadcasted_iota(jnp.int32, (ROWS, listed), 0)).astype(F32)
    place = c + (TOP + COUNT_LANE - 256)
    third = (place == lax.broadcasted_iota(jnp.int32, (128, listed), 0)).astype(F32)
    counts = nt(pair.astype(BF16), third.astype(BF16))
    out_ref[:, :, 0:256] = jnp.broadcast_to(total[:, 0:256], (out_ref.shape[0], ROWS, 256))
    out_ref[:, :, 256:384] = jnp.broadcast_to(total[:, 256:384] + counts, (out_ref.shape[0], ROWS, 128))


def weigh_kernel(scale, copies, tile_ref, part_ref, out_ref):
    total = jnp.sum(part_ref[...], axis=0)
    tile = tile_ref[0]
    row = lax.broadcasted_iota(jnp.int32, (ROWS, LANES), 0)
    lane = lax.broadcasted_iota(jnp.int32, (ROWS, LANES), 1)
    inner = jnp.where(lane >= HALF, lane - HALF, lane)
    second = inner >= HALF // 2
    c = jnp.where(second, inner - HALF // 2, inner) >> 3
    late = tile - 21
    i = jnp.where(late >= 6, 2, jnp.where(late >= 3, 1, 0))
    j = late - 3 * i
    late_a = jnp.where(i == 2, 10, jnp.where(i == 1, 9, 0))
    rest = jnp.where(row == 1, 9, jnp.where(row == 2, 10, jnp.where(row == 3, -9, jnp.where(row == 4, -10, 0))))
    late_b = jnp.where(j == 0, row + 1, jnp.where(j == 1, -row - 1, rest))
    a = jnp.where(tile < 21, row + 1, late_a)
    b = jnp.where(tile < 21, tile - TOP, late_b)
    square = jnp.maximum(a * a + b * b + c * c, 1).astype(F32)
    weight = jnp.exp(-0.025 * square) / square * scale
    wide_lane = lax.broadcasted_iota(jnp.int32, (128, LANES), 1)
    wide_inner = jnp.where(wide_lane >= HALF, wide_lane - HALF, wide_lane)
    wide_c = jnp.where(wide_inner >= HALF // 2, wide_inner - HALF // 2, wide_inner) >> 3
    offset = lax.broadcasted_iota(jnp.int32, (128, LANES), 0) - (TOP + COUNT_LANE - 256)
    live = wide_lane < COUNT_LANE
    plus = (live & (offset == wide_c)).astype(F32)
    minus = (live & (offset == -wide_c) & (wide_c > 0)).astype(F32)
    counts = total[:, 256:384].astype(BF16)
    both = nn(counts, (plus + minus).astype(BF16)) * (1.0 / copies)
    differ = nn(counts, (plus - minus).astype(BF16)) * (1.0 / copies)
    partner = jnp.where(lane < HALF, pltpu.roll(total, LANES - HALF, 1), pltpu.roll(total, HALF, 1))
    differ = jnp.where(second, differ, -differ)
    out = weight * (both * total + differ * partner)
    out_ref[...] = jnp.broadcast_to(out, out_ref.shape)


def apply_kernel(pos_ref, chg_ref, w_ref, energy_ref, force_ref, real_ref, imag_ref):
    charges = chg_ref[...]
    atoms = charges.shape[1]
    cx, sx = table(pos_ref[0:1, :])
    cy, sy = table(pos_ref[1:2, :])
    cz, sz = table(pos_ref[2:3, :])
    cq = z_rows(cz, charges)
    sq = z_rows(sz, charges)
    dc = [n * sq[n] for n in range(TOP + 1)]
    ds = [-n * cq[n] for n in range(TOP + 1)]
    blank = lambda n: [jnp.zeros((n, atoms), F32)]
    w = w_ref[...].reshape(TILES * ROWS, LANES)
    w_hi, w_lo = split(w)
    first, last = slice(0, 256), slice(128, 384)
    both = lambda one, two: split(jnp.concatenate([jnp.concatenate(one, axis=0), jnp.concatenate(two, axis=0)], axis=1))
    real_ref[...] = product(
        nn, (w_hi[:, first], w_lo[:, first]), both(cq + sq + blank(80), dc + ds + blank(80))
    )
    imag_ref[...] = product(
        nn,
        (w_hi[:, last], w_lo[:, last]),
        both(blank(48) + sq + cq + blank(32), blank(48) + ds + dc + blank(32)),
    )
    zero = jnp.zeros((8, atoms), F32)
    energy, along_z, ordinary, along_y = zero, zero, zero, zero
    side_x, up_y, rest_y = zero, zero, zero
    for tile in range(30):
        re, im = pair_tile(tile, cx, sx, cy, sy)
        rows = slice(8 * tile, 8 * tile + 8)
        g, h = real_ref[rows, 0:atoms], imag_ref[rows, 0:atoms]
        energy = energy + (re * g + im * h)
        along_z = along_z + (re * real_ref[rows, atoms : 2 * atoms] + im * imag_ref[rows, atoms : 2 * atoms])
        d = im * g - re * h
        if tile < 21:
            ordinary = ordinary + d
            along_y = along_y + (tile - TOP) * d
        else:
            i, j = divmod(tile - 21, 3)
            side_x = side_x + (0.0, 9.0, 10.0)[i] * d
            if j == 0:
                up_y = up_y + d
            elif j == 1:
                up_y = up_y - d
            else:
                rest_y = rest_y + d
    n = orders((16, atoms))
    along_x = ordinary * n[0:8] + side_x
    along_y = along_y + up_y * n[0:8] + rest_y * n[8:16]
    down = lambda v: jnp.sum(v, axis=0, keepdims=True)
    energy_ref[...] = 0.25 * down(energy)
    force_ref[0:1, :] = 0.1 * down(along_x)
    force_ref[1:2, :] = 0.1 * down(along_y)
    force_ref[2:3, :] = 0.1 * down(along_z)


def call(kernel, out_shape, scratch=(), scalar=False, operands=2):
    vmem = pl.BlockSpec(memory_space=pltpu.VMEM)
    in_specs = [vmem] * operands
    if scalar:
        in_specs = [pl.BlockSpec(memory_space=pltpu.SMEM)] + in_specs
    return pl.pallas_call(
        kernel,
        out_shape=out_shape,
        in_specs=in_specs,
        out_specs=jax.tree.map(lambda _: vmem, out_shape),
        scratch_shapes=list(scratch),
        compiler_params=pltpu.CompilerParams(vmem_limit_bytes=32 * 1024 * 1024),
    )


def per_device(scale, positions, charges, miller):
    atoms = positions.shape[1]
    column = lax.axis_size(COLUMN)
    shape = lambda *s: jax.ShapeDtypeStruct(s, F32)
    tile = lax.axis_index(SPREAD).astype(jnp.int32).reshape(1)
    pairs = (TILES * ROWS, atoms)
    part = call(struct_kernel, shape(TILES, ROWS, LANES), [pltpu.VMEM(pairs, BF16)] * 4)(positions, charges)
    part = lax.all_to_all(part, SPREAD, 0, 0, tiled=True)
    part = call(collect_kernel, shape(column, ROWS, LANES), scalar=True)(tile, part, miller)
    part = lax.all_to_all(part, COLUMN, 0, 0, tiled=True)
    copies = lax.axis_size("zh")
    weigh = functools.partial(weigh_kernel, scale, copies)
    w = call(weigh, shape(TILES, ROWS, LANES), scalar=True, operands=1)(tile, part)
    w = lax.all_to_all(w, SPREAD, 0, 0, tiled=True)
    wide = (TILES * ROWS, 2 * atoms)
    energy, force = call(
        apply_kernel, (shape(1, atoms), shape(3, atoms)), [pltpu.VMEM(wide, F32)] * 2, operands=3
    )(positions, charges, w)
    return energy.reshape(atoms), force


def solution(mesh):
    fine = Mesh(mesh.devices.reshape(8, 4, 2, 4, 2), ("zl", "y", "zh", "x", "c"))
    every = fine.axis_names
    in_specs = (P(None, every), P(None, every), P(None, "zl"))
    out_specs = (P(every), P(None, every))

    def run(positions, charges, miller):
        scale = 1.0 / float(positions.shape[1]) ** 0.5
        body = functools.partial(per_device, scale)
        return jax.shard_map(body, mesh=fine, in_specs=in_specs, out_specs=out_specs, check_vma=False)(
            positions, charges, miller
        )

    return run
```

time: 907 us -> 71.4 us (0.08)
  the two profiles are of different devices: /device:TPU:32 before, /device:TPU:1 now
where the time goes in v1:
time: 71.4 us; the launch traced here: 71 us
  blocking collectives  44.5 us (62%)
  starting transfers between devices  10.4 us (15%)
  waiting for transfers between devices  10.3 us (14%)
  Pallas kernels  3.75 us (5%)
  local copies, waits for them, and re-layouts  1.43 us (2%)
    all_to_all x1, blocking collectives, per_device(): part = lax.all_to_all(part, COLUMN, 0, 0, tiled=True)  28.2 us
    all_to_all x1, blocking collectives, per_device(): w = lax.all_to_all(w, SPREAD, 0, 0, tiled=True)  16.3 us
    all_to_all x1, starting transfers between devices, per_device(): part = lax.all_to_all(part, SPREAD, 0, 0, tiled=True)  10.4 us
    all_to_all x1, waiting for transfers between devices, per_device(): part = lax.all_to_all(part, SPREAD, 0, 0, tiled=True)  10.3 us
    pallas_call x1, Pallas kernels, per_device(): call(apply_kernel, (shape(1, atoms), shape(3, atoms)), [pltpu.VMEM(wide,...  1.85 us
    pallas_call x1, Pallas kernels, per_device(): call(struct_kernel, shape(TILES, ROWS, LANES), [pltpu.VMEM(pairs, BF16)]...  1.51 us
  transfers between devices with their start and end apart: 1, of which 1 were waited for; matrix products, arithmetic and copies ran while one was open for 0% of the time, Pallas kernels for 0%

profile of v1, /device:TPU:1, one launch (start us, length us, event | category | flops | bytes accessed | tf_op | source)
XLA Modules:
  0.0 71.0 jit_solution(5730221249033174684)
XLA Ops:
  0.6 0.0 copy-start
  0.6 0.7 copy-done
  1.3 0.0 copy-start.2
  1.4 0.7 copy-done.2
  2.0 1.5 %shard_map.50 = f32[32,8,384]{2,1,0:T(8,128)} custom-call(f32[3,512]{1,0:T(4,128)S(1)} %copy-done.2, f32[8,512]{1,0:T(8,128)S(1)} %copy-done), custom_call_target="tpu_custom_call" | custom-call | tf_op jit(solution)/shard_map/pallas_call | solution.py:261
  3.6 10.4 %all-to-all-start = ((f32[32,8,384]{2,1,0:T(8,128)}), f32[32,8,384]{2,1,0:T(8,128)S(1)}, u32[]{:S(2)}, u32[]{:S(2)}) async-start(f32[32,8,384]{2,1,0:T(8,128)} %shard_map.50), calls=%async_computation | async-start | bytes 786432 | tf_op jit(solution)/shard_map/all_to_all | solution.py:262
  14.0 0.0 copy-start.4
  14.0 10.3 %all-to-all-done.part_ref = f32[32,8,384]{2,1,0:T(8,128)S(1)} async-done(((f32[32,8,384]{2,1,0:T(8,128)}), f32[32,8,384]{2,1,0:T(8,128)S(1)}, u32[]{:S(2)}, u32[]{:S(2)}) %all-to-all-start) | async-done | bytes 393248 | tf_op jit(solution)/shard_map/all_to_all | solution.py:262
  24.3 0.0 copy-done.4
  24.3 0.2 shard_map.51
  24.4 28.2 %all_to_all.15.part_ref = f32[16,8,384]{2,1,0:T(8,128)S(1)} all-to-all(f32[16,8,384]{2,1,0:T(8,128)S(1)} %shard_map.51), channel_id=1, replica_groups=mesh['zl'=8,'y'=4,'zh'=2,'x'=4,'c'=2] {'zl','zh'}, dimensions={0} | all-to-all | bytes 393216 | tf_op jit(solution)/shard_map/all_to_all | solution.py:264
  52.6 0.2 shard_map.52
  52.8 0.0 copy-start.1
  52.8 0.0 copy-start.3
  52.9 16.3 %all_to_all.16.w_ref = f32[32,8,384]{2,1,0:T(8,128)S(1)} all-to-all(f32[32,8,384]{2,1,0:T(8,128)S(1)} %shard_map.52), channel_id=1, replica_groups=mesh['zl'=8,'y'=4,'zh'=2,'x'=4,'c'=2] {'y','x','c'}, dimensions={0} | all-to-all | bytes 786432 | tf_op jit(solution)/shard_map/all_to_all | solution.py:268
  69.2 0.0 copy-done.1
  69.2 0.0 copy-done.3
  69.2 1.9 %shard_map.53 = (f32[1,512]{1,0:T(1,128)}, f32[3,512]{1,0:T(4,128)}) custom-call(f32[3,512]{1,0:T(4,128)S(1)} %copy-done.3, f32[8,512]{1,0:T(8,128)S(1)} %copy-done.1, f32[32,8,384]{2,1,0:T(8,128)S(1)} %all_to_all.16.w_ref), custom_call_target="tpu_custom_call" | custom-call | tf_op jit(solution)/shard_map/pallas_call | solution.py:270
Async XLA Ops:
  0.6 0.7 %copy-start = (f32[8,512]{1,0:T(8,128)S(1)}, f32[8,512]{1,0:T(8,128)}, u32[]{:S(2)}) copy-start(f32[8,512]{1,0:T(8,128)} %chg_ref.3) | copy-start | bytes 49156
  1.3 0.7 copy-start.2
  3.6 20.7 %all-to-all-start = ((f32[32,8,384]{2,1,0:T(8,128)}), f32[32,8,384]{2,1,0:T(8,128)S(1)}, u32[]{:S(2)}, u32[]{:S(2)}) async-start(f32[32,8,384]{2,1,0:T(8,128)} %shard_map.50), calls=%async_computation | async-start | bytes 786432 | tf_op jit(solution)/shard_map/all_to_all | solution.py:262
  14.0 10.3 %copy-start.4 = (s32[3,512]{1,0:T(4,128)S(1)}, s32[3,512]{1,0:T(4,128)}, u32[]{:S(2)}) copy-start(s32[3,512]{1,0:T(4,128)} %miller_ref.1) | copy-start | bytes 18436
  52.8 16.4 %copy-start.1 = (f32[8,512]{1,0:T(8,128)S(1)}, f32[8,512]{1,0:T(8,128)}, u32[]{:S(2)}) copy-start(f32[8,512]{1,0:T(8,128)} %chg_ref.3) | copy-start | bytes 49156
  52.8 16.4 %copy-start.3 = (f32[3,512]{1,0:T(4,128)S(1)}, f32[3,512]{1,0:T(4,128)}, u32[]{:S(2)}) copy-start(f32[3,512]{1,0:T(4,128)} %pos_ref.3) | copy-start | bytes 18436

commit v2 on v1

v2 whole, which is shorter than its diff:
```python
import functools

import jax
import jax.numpy as jnp
import numpy as np
from jax import lax
from jax.experimental import pallas as pl
from jax.experimental.pallas import tpu as pltpu
from jax.sharding import Mesh
from jax.sharding import PartitionSpec as P

TOP = 10
TILES = 16
ROWS = 8
USED = 7
HALF = 176
LANES = 384
COUNT_LANE = 352
SIN = (3.141592640130706, -5.167710083507839, 2.550077523214083, -0.5982912856178239, 0.07765766030006041)
COS = (
    1.0,
    -4.934802137078852,
    4.058709159556494,
    -1.3352120030499017,
    0.23493731380758293,
    -0.02439632432974524,
)
F32 = jnp.float32
BF16 = jnp.bfloat16
SHAPE = (8, 4, 2, 4, 2)
AXES = ("zl", "y", "zh", "x", "c")


def column_groups():
    ids = np.arange(512).reshape(SHAPE)
    order = [(8 + n // 2 + 8 * (n % 2)) % 16 for n in range(16)]
    return [[int(ids[z % 8, y, z // 8, x, c]) for z in order] for y in range(4) for x in range(4) for c in range(2)]


def horner(coefs, u):
    out = jnp.full_like(u, coefs[-1])
    for c in coefs[-2::-1]:
        out = out * u + c
    return out


def cos_sin(turns):
    t = turns - jnp.round(turns)
    u = t * t
    s = t * horner(SIN, u)
    return 1.0 - 2.0 * s * s, 2.0 * s * horner(COS, u)


def table(coordinate):
    r = lax.broadcasted_iota(jnp.int32, (16, coordinate.shape[1]), 0)
    return cos_sin(jnp.where(r < TOP, r + 1, 0).astype(F32) * coordinate)


def late_orders(core, lanes):
    q = lax.broadcasted_iota(jnp.int32, (24, lanes), 0)
    n = jnp.where(q < 7, q, jnp.where((q >= 8) & (q < 12), q - 1, 0))
    late_a = jnp.where((q >= 12) & (q < 15), 8, jnp.where((q >= 16) & (q < 19), 9, jnp.where((q >= 19) & (q < 22), 10, 0)))
    late_b = jnp.where(late_a == 8, q - 4, jnp.where(late_a == 9, q - 8, jnp.where(late_a == 10, q - 11, 0)))
    return jnp.where(core == 0, n + late_a, late_a).astype(F32), jnp.where(core == 0, late_b, n + late_b).astype(F32)


def split(x):
    high = x.astype(BF16)
    return high, (x - high.astype(F32)).astype(BF16)


def factors(tile, cx, sx, cy, sy):
    if tile < 10:
        ca, sa, cb, sb = cx[0:8], sx[0:8], cy[tile : tile + 1], sy[tile : tile + 1]
    else:
        r = tile - 3
        ca, sa, cb, sb = cx[r : r + 1], sx[r : r + 1], cy[0:8], sy[0:8]
    return ca * cb, sa * sb, sa * cb, ca * sb


def z_rows(rows, first, charges):
    return [first] + [rows[n : n + 1] * charges for n in range(TOP)]


def nt(a, b):
    return lax.dot_general(a, b, (((1,), (1,)), ((), ())), preferred_element_type=F32)


def nn(a, b):
    return jnp.dot(a, b, preferred_element_type=F32)


def product(mul, a, b):
    return mul(a[0], b[0]) + (mul(a[0], b[1]) + mul(a[1], b[0]))


def stack(*parts):
    return jnp.concatenate([p for part in parts for p in part], axis=0)


def struct_kernel(core_ref, atoms_ref, out_ref, re_hi, re_lo, im_hi, im_lo):
    core = core_ref[0]
    both = jnp.concatenate([atoms_ref[0], atoms_ref[1]], axis=1)
    lanes = both.shape[1]
    x, z, charges = both[0:1], both[2:3], both[3:11]
    y = both[1:2] * jnp.where(core == 0, 1.0, -1.0)
    cx, sx = table(x)
    cy, sy = table(y)
    cz, sz = table(z)
    a, b = late_orders(core, lanes)
    late_c, late_s = cos_sin(a * x + b * y)
    for two in range(TILES // 2):
        real, imag = [], []
        for tile in (2 * two, 2 * two + 1):
            if tile < 13:
                cc, ss, sc, cs = factors(tile, cx, sx, cy, sy)
                real.append(cc - ss)
                imag.append(sc + cs)
            else:
                rows = slice(8 * (tile - 13), 8 * (tile - 12))
                real.append(late_c[rows])
                imag.append(late_s[rows])
        rows = slice(16 * two, 16 * two + 16)
        re_hi[rows, :], re_lo[rows, :] = split(stack(real))
        im_hi[rows, :], im_lo[rows, :] = split(stack(imag))
    cq = z_rows(cz, charges, charges)
    sq = z_rows(sz, jnp.zeros_like(charges), charges)
    blank = lambda n: [jnp.zeros((n, lanes), F32)]
    real = product(nt, (re_hi[...], re_lo[...]), split(stack(cq, sq, blank(80))))
    imag = product(nt, (im_hi[...], im_lo[...]), split(stack(blank(48), sq, cq, blank(32))))
    out_ref[:, :, 0:128] = real[:, 0:128].reshape(TILES, ROWS, 128)
    out_ref[:, :, 128:256] = (real[:, 128:256] + imag[:, 0:128]).reshape(TILES, ROWS, 128)
    out_ref[:, :, 256:384] = imag[:, 128:256].reshape(TILES, ROWS, 128)


def place_of(a, b):
    core = jnp.where(b < 0, 1, 0)
    b = jnp.abs(b)
    n = a + b
    axis = jnp.where(n <= 6, 13 * 8 + n, 14 * 8 + n - 7)
    corner = jnp.where(a == 8, 14 * 8 + b - 4, 15 * 8 + (a - 9) * 3 + b - 8)
    rest = jnp.where(a <= 7, (b - 1) * 8 + a - 1, jnp.where(b <= 7, (a + 2) * 8 + b - 1, corner))
    return core * (TILES * ROWS) + jnp.where((a == 0) | (b == 0), axis, rest)


def collect_kernel(place_ref, part_ref, miller_ref, out_ref):
    total = jnp.sum(part_ref[...], axis=0)
    a, b, c = miller_ref[0:1, :], miller_ref[1:2, :], miller_ref[2:3, :]
    sign = jnp.where((a < 0) | ((a == 0) & (b > 0)), -1, 1)
    a, b, c = a * sign, b * sign, c * sign
    listed = a.shape[1]
    row = place_of(a, b) - place_ref[0]
    pair = (row == lax.broadcasted_iota(jnp.int32, (ROWS, listed), 0)).astype(F32)
    lane = c + (TOP + COUNT_LANE - 256)
    third = (lane == lax.broadcasted_iota(jnp.int32, (128, listed), 0)).astype(F32)
    counts = nt(pair.astype(BF16), third.astype(BF16))
    copies = out_ref.shape[0]
    for r in range(USED):
        out_ref[:, :, LANES * r : LANES * r + 256] = jnp.broadcast_to(total[r : r + 1, 0:256], (copies, 1, 256))
        last = total[r : r + 1, 256:384] + counts[r : r + 1]
        out_ref[:, :, LANES * r + 256 : LANES * r + 384] = jnp.broadcast_to(last, (copies, 1, 128))


def weigh_kernel(scale, copies, tile_ref, part_ref, out_ref):
    flat = jnp.sum(part_ref[...], axis=0)
    total = stack([flat[:, LANES * r : LANES * r + LANES] for r in range(USED)], [jnp.zeros((1, LANES), F32)])
    tile = tile_ref[0]
    row = lax.broadcasted_iota(jnp.int32, (ROWS, LANES), 0)
    lane = lax.broadcasted_iota(jnp.int32, (ROWS, LANES), 1)
    inner = jnp.where(lane >= HALF, lane - HALF, lane)
    second = inner >= HALF // 2
    c = jnp.where(second, inner - HALF // 2, inner) >> 3
    a = jnp.where(tile < 10, tile + 1, jnp.where(tile < 13, tile - 2, 0))
    b = row + 1
    a = jnp.where(tile == 13, 0, jnp.where(tile == 14, jnp.where(row < 4, 0, 8), a))
    b = jnp.where(tile == 13, row, jnp.where(tile == 14, jnp.where(row < 4, row + 7, row + 4), b))
    a = jnp.where(tile == 15, jnp.where(row < 3, 9, 10), a)
    b = jnp.where(tile == 15, jnp.where(row < 3, row + 8, row + 5), b)
    square = jnp.maximum(a * a + b * b + c * c, 1).astype(F32)
    weight = jnp.exp(-0.025 * square) / square * scale
    wide_lane = lax.broadcasted_iota(jnp.int32, (128, LANES), 1)
    wide_inner = jnp.where(wide_lane >= HALF, wide_lane - HALF, wide_lane)
    wide_c = jnp.where(wide_inner >= HALF // 2, wide_inner - HALF // 2, wide_inner) >> 3
    offset = lax.broadcasted_iota(jnp.int32, (128, LANES), 0) - (TOP + COUNT_LANE - 256)
    live = wide_lane < COUNT_LANE
    plus = (live & (offset == wide_c)).astype(F32)
    minus = (live & (offset == -wide_c) & (wide_c > 0)).astype(F32)
    counts = total[:, 256:384].astype(BF16)
    both = nn(counts, (plus + minus).astype(BF16)) * (1.0 / copies)
    differ = nn(counts, (plus - minus).astype(BF16)) * (1.0 / copies)
    partner = jnp.where(lane < HALF, pltpu.roll(total, LANES - HALF, 1), pltpu.roll(total, HALF, 1))
    differ = jnp.where(second, differ, -differ)
    out = weight * (both * total + differ * partner)
    out_ref[...] = jnp.broadcast_to(out, out_ref.shape)


def apply_kernel(atoms_ref, w_ref, energy_ref, force_ref, real_ref, imag_ref):
    x, y, z, charges = atoms_ref[0:1, :], atoms_ref[1:2, :], atoms_ref[2:3, :], atoms_ref[3:11, :]
    atoms = x.shape[1]
    cx, sx = table(x)
    cy, sy = table(y)
    cz, sz = table(z)
    none = jnp.zeros_like(charges)
    cq = z_rows(cz, charges, charges)
    sq = z_rows(sz, none, charges)
    dc = [n * sq[n] for n in range(TOP + 1)]
    ds = [-n * cq[n] for n in range(TOP + 1)]
    blank = lambda n: [jnp.zeros((n, atoms), F32)]
    w_hi, w_lo = split(w_ref[...].reshape(2 * TILES * ROWS, LANES))
    first, last = slice(0, 256), slice(128, 384)
    beside = lambda one, two: split(jnp.concatenate([stack(*one), stack(*two)], axis=1))
    real_ref[...] = product(
        nn, (w_hi[:, first], w_lo[:, first]), beside((cq, sq, blank(80)), (dc, ds, blank(80)))
    )
    imag_ref[...] = product(
        nn,
        (w_hi[:, last], w_lo[:, last]),
        beside((blank(48), sq, cq, blank(32)), (blank(48), ds, dc, blank(32))),
    )
    zero = jnp.zeros((8, atoms), F32)
    sums = {"e": zero, "z": zero, "x": zero, "y": zero, "x_row": zero, "y_row": zero}

    def add(core, tile, re, im):
        rows = slice(8 * (core * TILES + tile), 8 * (core * TILES + tile) + 8)
        g, h = real_ref[rows, 0:atoms], imag_ref[rows, 0:atoms]
        sums["e"] += re * g + im * h
        sums["z"] += re * real_ref[rows, atoms : 2 * atoms] + im * imag_ref[rows, atoms : 2 * atoms]
        return im * g - re * h

    for tile in range(13):
        cc, ss, sc, cs = factors(tile, cx, sx, cy, sy)
        up, down = add(0, tile, cc - ss, sc + cs), add(1, tile, cc + ss, sc - cs)
        if tile < 10:
            sums["x_row"] += up + down
            sums["y"] += (tile + 1.0) * (up - down)
        else:
            sums["x"] += (tile - 2.0) * (up + down)
            sums["y_row"] += up - down
    for core in range(2):
        a, b = late_orders(core, atoms)
        b = b * (1.0 - 2.0 * core)
        late_c, late_s = cos_sin(a * x + b * y)
        for j in range(3):
            rows = slice(8 * j, 8 * j + 8)
            d = add(core, 13 + j, late_c[rows], late_s[rows])
            sums["x"] += a[rows] * d
            sums["y"] += b[rows] * d
    order = lax.broadcasted_iota(jnp.int32, (8, atoms), 0).astype(F32) + 1.0
    down = lambda v: jnp.sum(v, axis=0, keepdims=True)
    energy_ref[...] = 0.25 * down(sums["e"])
    force_ref[0:1, :] = 0.1 * down(sums["x"] + order * sums["x_row"])
    force_ref[1:2, :] = 0.1 * down(sums["y"] + order * sums["y_row"])
    force_ref[2:3, :] = 0.1 * down(sums["z"])


def call(kernel, out_shape, operands, scratch=(), scalar=False):
    vmem = pl.BlockSpec(memory_space=pltpu.VMEM)
    in_specs = [vmem] * operands
    if scalar:
        in_specs = [pl.BlockSpec(memory_space=pltpu.SMEM)] + in_specs
    return pl.pallas_call(
        kernel,
        out_shape=out_shape,
        in_specs=in_specs,
        out_specs=jax.tree.map(lambda _: vmem, out_shape),
        scratch_shapes=list(scratch),
        compiler_params=pltpu.CompilerParams(vmem_limit_bytes=32 * 1024 * 1024),
    )


def per_device(scale, positions, charges, miller):
    atoms = positions.shape[1]
    column = lax.axis_size("zl") * lax.axis_size("zh")
    copies = lax.axis_size("zh")
    shape = lambda *s: jax.ShapeDtypeStruct(s, F32)
    core = lax.axis_index("c").astype(jnp.int32).reshape(1)
    tile = lax.axis_index(("y", "x")).astype(jnp.int32).reshape(1)
    place = core * (TILES * ROWS) + tile * ROWS
    own = jnp.concatenate([positions, charges], axis=0)
    pair = lax.all_gather(own, "c")
    half = [pltpu.VMEM((TILES * ROWS, 2 * atoms), BF16)] * 4
    part = call(struct_kernel, shape(TILES, ROWS, LANES), 1, half, scalar=True)(core, pair)
    part = lax.all_to_all(part, ("y", "x"), 0, 0, tiled=True)
    part = call(collect_kernel, shape(column, 1, USED * LANES), 2, scalar=True)(place, part, miller)
    part = lax.all_to_all(part, AXES, 0, 0, axis_index_groups=column_groups(), tiled=True)
    weigh = functools.partial(weigh_kernel, scale, copies)
    w = call(weigh, shape(TILES, ROWS, LANES), 1, scalar=True)(tile, part)
    w = lax.all_to_all(w, ("y", "x"), 0, 0, tiled=True)
    w = lax.all_gather(w, "c")
    wide = [pltpu.VMEM((2 * TILES * ROWS, 2 * atoms), F32)] * 2
    energy, force = call(apply_kernel, (shape(1, atoms), shape(3, atoms)), 2, wide)(own, w)
    return energy.reshape(atoms), force


def solution(mesh):
    fine = Mesh(mesh.devices.reshape(SHAPE), AXES)
    in_specs = (P(None, AXES), P(None, AXES), P(None, "zl"))
    out_specs = (P(AXES), P(None, AXES))

    def run(positions, charges, miller):
        scale = 1.0 / float(positions.shape[1]) ** 0.5
        body = functools.partial(per_device, scale)
        return jax.shard_map(body, mesh=fine, in_specs=in_specs, out_specs=out_specs, check_vma=False)(
            positions, charges, miller
        )

    return run
```

time: 71.4 us -> 63.1 us (0.88)
  starting transfers between devices: 10.4 us -> 3.52 us
  waiting for transfers between devices: 10.3 us -> 7.68 us
  local copies, waits for them, and re-layouts: 1.43 us -> 0.01 us
  blocking collectives: 44.5 us -> 45.6 us
  other arithmetic: 0 us -> 0.73 us
    all_gather x0 -> x2, blocking collectives: none -> 13.6 us  [the longest x1 8.38 us: per_device(): pair = lax.all_gather(own, 'c')]
    all_to_all x2, blocking collectives: 44.5 us -> 32.1 us  [the longest x1 19.7 us: per_device(): lax.all_to_all(part, AXES, 0, 0, axis_index_groups=column_groups(), tiled...]
    all_to_all x1, starting transfers between devices: 10.4 us -> 3.52 us  [per_device(): part = lax.all_to_all(part, ('y', 'x'), 0, 0, tiled=True)]
    all_to_all x1, waiting for transfers between devices: 10.3 us -> 7.68 us  [per_device(): part = lax.all_to_all(part, ('y', 'x'), 0, 0, tiled=True)]
    unnamed x10 -> x2, local copies, waits for them, and re-layouts: 1.43 us -> 0.01 us
    unnamed x0 -> x1, other arithmetic: none -> 0.73 us
where the time goes in v2:
time: 63.1 us; the launch traced here: 62.7 us
  blocking collectives  45.6 us (72%)
  waiting for transfers between devices  7.68 us (12%)
  Pallas kernels  4.41 us (7%)
  starting transfers between devices  3.52 us (6%)
  other arithmetic  0.73 us (1%)
  between operations  0.68 us (1%)
    all_to_all x1, blocking collectives, per_device(): lax.all_to_all(part, AXES, 0, 0, axis_index_groups=column_groups(), tiled...  19.7 us
    all_to_all x1, blocking collectives, per_device(): w = lax.all_to_all(w, ('y', 'x'), 0, 0, tiled=True)  12.4 us
    all_gather x1, blocking collectives, per_device(): pair = lax.all_gather(own, 'c')  8.38 us
    all_to_all x1, waiting for transfers between devices, per_device(): part = lax.all_to_all(part, ('y', 'x'), 0, 0, tiled=True)  7.68 us
    all_gather x1, blocking collectives, per_device(): w = lax.all_gather(w, 'c')  5.17 us
    all_to_all x1, starting transfers between devices, per_device(): part = lax.all_to_all(part, ('y', 'x'), 0, 0, tiled=True)  3.52 us
    pallas_call x1, Pallas kernels, per_device(): call(struct_kernel, shape(TILES, ROWS, LANES), 1, half, scalar=True)  1.99 us
    pallas_call x1, Pallas kernels, per_device(): call(apply_kernel, (shape(1, atoms), shape(3, atoms)), 2, wide)(own, w)  1.99 us
  transfers between devices with their start and end apart: 1, of which 1 were waited for; matrix products, arithmetic and copies ran while one was open for 0% of the time, Pallas kernels for 0%

profile of v2, /device:TPU:1, one launch (start us, length us, event | category | flops | bytes accessed | tf_op | source)
XLA Modules:
  0.0 62.7 jit_solution(6287858162170965582)
XLA Ops:
  0.6 0.7 %fusion = (f32[1,11,512]{2,1,0:T(8,128)S(1)}, f32[11,512]{1,0:T(8,128)S(1)}) fusion(f32[8,512]{1,0:T(8,128)} %param.4, f32[3,512]{1,0:T(4,128)} %param.3), kind=kLoop, calls=%fused_computation.1 | loop fusion | flops 5632 | bytes 67584
  1.4 8.4 %all-gather.2.atoms_ref = f32[2,11,512]{2,1,0:T(8,128)S(1)} all-gather(f32[1,11,512]{2,1,0:T(8,128)S(1)} %get-tuple-element.6), channel_id=2, replica_groups=mesh['zl'=8,'y'=4,'zh'=2,'x'=4,'c'=2] {'c'}, dimensions={0}, use_global_device_ids=true | all-gather | bytes 67584 | tf_op jit(solution)/shard_map/all_gather | solution.py:280
  9.7 2.0 %shard_map.50 = f32[16,8,384]{2,1,0:T(8,128)} custom-call(s32[1]{0:T(128)} %bitcast.1.core_ref, f32[2,11,512]{2,1,0:T(8,128)S(1)} %all-gather.2.atoms_ref), custom_call_target="tpu_custom_call" | custom-call | tf_op jit(solution)/shard_map/pallas_call | solution.py:282
  11.7 3.5 %all-to-all-start = ((f32[16,8,384]{2,1,0:T(8,128)}), f32[16,8,384]{2,1,0:T(8,128)S(1)}, u32[]{:S(2)}, u32[]{:S(2)}) async-start(f32[16,8,384]{2,1,0:T(8,128)} %shard_map.50), calls=%async_computation | async-start | bytes 393216 | tf_op jit(solution)/shard_map/all_to_all | solution.py:283
  15.3 0.0 copy-start
  15.3 7.7 %all-to-all-done.part_ref = f32[16,8,384]{2,1,0:T(8,128)S(1)} async-done(((f32[16,8,384]{2,1,0:T(8,128)}), f32[16,8,384]{2,1,0:T(8,128)S(1)}, u32[]{:S(2)}, u32[]{:S(2)}) %all-to-all-start) | async-done | bytes 196640 | tf_op jit(solution)/shard_map/all_to_all | solution.py:283
  23.0 0.0 copy-done
  23.0 0.2 shard_map.51
  23.2 19.7 %all_to_all.15.part_ref = f32[16,1,2688]{2,1,0:T(1,128)S(1)} all-to-all(f32[16,1,2688]{2,1,0:T(1,128)S(1)} %shard_map.51), channel_id=1, replica_groups={{8,0,72,64,136,128,200,192,264,256,328,320,392,384,456,448},{9,1,73,65,..., dimensions={0} | all-to-all | bytes 344064 | tf_op jit(solution)/shard_map/all_to_all | solution.py:285
  42.9 0.2 shard_map.52
  43.2 12.4 %all_to_all.16 = f32[16,8,384]{2,1,0:T(8,128)S(1)} all-to-all(f32[16,8,384]{2,1,0:T(8,128)S(1)} %shard_map.52), channel_id=1, replica_groups=mesh['zl'=8,'y'=4,'zh'=2,'x'=4,'c'=2] {'y','x'}, dimensions={0} | all-to-all | bytes 393216 | tf_op jit(solution)/shard_map/all_to_all | solution.py:288
  55.5 5.2 %all-gather.1 = f32[32,8,384]{2,1,0:T(8,128)S(1)} all-gather(f32[16,8,384]{2,1,0:T(8,128)S(1)} %all_to_all.16), channel_id=3, replica_groups=mesh['zl'=8,'y'=4,'zh'=2,'x'=4,'c'=2] {'c'}, dimensions={0}, use_global_device_ids=true | all-gather | bytes 589824 | tf_op jit(solution)/shard_map/all_gather | solution.py:289
  60.7 2.0 %shard_map.53 = (f32[1,512]{1,0:T(1,128)}, f32[3,512]{1,0:T(4,128)}) custom-call(f32[11,512]{1,0:T(8,128)S(1)} %get-tuple-element.7.atoms_ref, f32[2,16,8,384]{3,2,1,0:T(8,128)S(1)} %bitcast.6), custom_call_target="tpu_custom_call" | custom-call | tf_op jit(solution)/shard_map/pallas_call | solution.py:291
Async XLA Ops:
  11.7 11.2 %all-to-all-start = ((f32[16,8,384]{2,1,0:T(8,128)}), f32[16,8,384]{2,1,0:T(8,128)S(1)}, u32[]{:S(2)}, u32[]{:S(2)}) async-start(f32[16,8,384]{2,1,0:T(8,128)} %shard_map.50), calls=%async_computation | async-start | bytes 393216 | tf_op jit(solution)/shard_map/all_to_all | solution.py:283
  15.3 7.7 %copy-start = (s32[3,512]{1,0:T(4,128)S(1)}, s32[3,512]{1,0:T(4,128)}, u32[]{:S(2)}) copy-start(s32[3,512]{1,0:T(4,128)} %miller_ref.1) | copy-start | bytes 18436

commit v3 on v2

--- a/solution.py
+++ b/solution.py
@@ -29,12 +29,20 @@
 BF16 = jnp.bfloat16
 SHAPE = (8, 4, 2, 4, 2)
 AXES = ("zl", "y", "zh", "x", "c")
+ROOT = (2, 2)
 
 
 def column_groups():
     ids = np.arange(512).reshape(SHAPE)
     order = [(8 + n // 2 + 8 * (n % 2)) % 16 for n in range(16)]
     return [[int(ids[z % 8, y, z // 8, x, c]) for z in order] for y in range(4) for x in range(4) for c in range(2)]
+
+
+def plane_groups():
+    ids = np.arange(512).reshape(SHAPE)
+    order = [((n // 4 + ROOT[0]) % 4, (n % 4 + ROOT[1]) % 4) for n in range(16)]
+    rest = [(zl, zh, c) for zl in range(8) for zh in range(2) for c in range(2)]
+    return [[int(ids[zl, y, zh, x, c]) for y, x in order] for zl, zh, c in rest]
 
 
 def horner(coefs, u):
@@ -90,25 +98,31 @@
     return jnp.dot(a, b, preferred_element_type=F32)
 
 
-def product(mul, a, b):
-    return mul(a[0], b[0]) + (mul(a[0], b[1]) + mul(a[1], b[0]))
-
-
 def stack(*parts):
     return jnp.concatenate([p for part in parts for p in part], axis=0)
 
 
-def struct_kernel(core_ref, atoms_ref, out_ref, re_hi, re_lo, im_hi, im_lo):
-    core = core_ref[0]
+def struct_kernel(place_ref, atoms_ref, out_ref, counts_ref, pairs_ref):
+    place = place_ref[0]
+    core = jnp.where(place < TILES * ROWS, 0, 1)
+    listed = [atoms_ref[0, r : r + 1, :].astype(jnp.int32) for r in (11, 12, 13)]
+    counts_ref[...] = count_listed(place, *listed)
     both = jnp.concatenate([atoms_ref[0], atoms_ref[1]], axis=1)
     lanes = both.shape[1]
-    x, z, charges = both[0:1], both[2:3], both[3:11]
-    y = both[1:2] * jnp.where(core == 0, 1.0, -1.0)
+    x, z, charges = both[8:9], both[10:11], both[0:8]
+    y = both[9:10] * jnp.where(core == 0, 1.0, -1.0)
     cx, sx = table(x)
     cy, sy = table(y)
     cz, sz = table(z)
     a, b = late_orders(core, lanes)
     late_c, late_s = cos_sin(a * x + b * y)
+
+    def keep(rows, value):
+        high, low = split(value)
+        pairs_ref[rows, 0:lanes] = high
+        pairs_ref[rows, lanes : 2 * lanes] = low
+        pairs_ref[rows, 2 * lanes : 3 * lanes] = high
+
     for two in range(TILES // 2):
         real, imag = [], []
         for tile in (2 * two, 2 * two + 1):
@@ -120,14 +134,13 @@
                 rows = slice(8 * (tile - 13), 8 * (tile - 12))
                 real.append(late_c[rows])
                 imag.append(late_s[rows])
-        rows = slice(16 * two, 16 * two + 16)
-        re_hi[rows, :], re_lo[rows, :] = split(stack(real))
-        im_hi[rows, :], im_lo[rows, :] = split(stack(imag))
+        keep(slice(16 * two, 16 * two + 16), stack(real))
+        keep(slice(128 + 16 * two, 128 + 16 * two + 16), stack(imag))
     cq = z_rows(cz, charges, charges)
     sq = z_rows(sz, jnp.zeros_like(charges), charges)
-    blank = lambda n: [jnp.zeros((n, lanes), F32)]
-    real = product(nt, (re_hi[...], re_lo[...]), split(stack(cq, sq, blank(80))))
-    imag = product(nt, (im_hi[...], im_lo[...]), split(stack(blank(48), sq, cq, blank(32))))
+    high, low = split(stack(cq, sq, [jnp.zeros((256 - HALF, lanes), F32)]))
+    sums = nt(pairs_ref[...], jnp.concatenate([high, high, low], axis=1))
+    real, imag = sums[0:128], pltpu.roll(sums[128:256], HALF - 128, 1)
     out_ref[:, :, 0:128] = real[:, 0:128].reshape(TILES, ROWS, 128)
     out_ref[:, :, 128:256] = (real[:, 128:256] + imag[:, 0:128]).reshape(TILES, ROWS, 128)
     out_ref[:, :, 256:384] = imag[:, 128:256].reshape(TILES, ROWS, 128)
@@ -143,21 +156,23 @@
     return core * (TILES * ROWS) + jnp.where((a == 0) | (b == 0), axis, rest)
 
 
-def collect_kernel(place_ref, part_ref, miller_ref, out_ref):
-    total = jnp.sum(part_ref[...], axis=0)
-    a, b, c = miller_ref[0:1, :], miller_ref[1:2, :], miller_ref[2:3, :]
+def count_listed(place, a, b, c):
     sign = jnp.where((a < 0) | ((a == 0) & (b > 0)), -1, 1)
     a, b, c = a * sign, b * sign, c * sign
     listed = a.shape[1]
-    row = place_of(a, b) - place_ref[0]
+    row = place_of(a, b) - place
     pair = (row == lax.broadcasted_iota(jnp.int32, (ROWS, listed), 0)).astype(F32)
     lane = c + (TOP + COUNT_LANE - 256)
     third = (lane == lax.broadcasted_iota(jnp.int32, (128, listed), 0)).astype(F32)
-    counts = nt(pair.astype(BF16), third.astype(BF16))
+    return nt(pair.astype(BF16), third.astype(BF16))
+
+
+def collect_kernel(part_ref, counts_ref, out_ref):
+    total = jnp.sum(part_ref[...], axis=0)
     copies = out_ref.shape[0]
     for r in range(USED):
         out_ref[:, :, LANES * r : LANES * r + 256] = jnp.broadcast_to(total[r : r + 1, 0:256], (copies, 1, 256))
-        last = total[r : r + 1, 256:384] + counts[r : r + 1]
+        last = total[r : r + 1, 256:384] + counts_ref[r : r + 1, :]
         out_ref[:, :, LANES * r + 256 : LANES * r + 384] = jnp.broadcast_to(last, (copies, 1, 128))
 
 
@@ -188,14 +203,17 @@
     counts = total[:, 256:384].astype(BF16)
     both = nn(counts, (plus + minus).astype(BF16)) * (1.0 / copies)
     differ = nn(counts, (plus - minus).astype(BF16)) * (1.0 / copies)
-    partner = jnp.where(lane < HALF, pltpu.roll(total, LANES - HALF, 1), pltpu.roll(total, HALF, 1))
-    differ = jnp.where(second, differ, -differ)
+    near, far = HALF // 2, HALF + HALF // 2
+    ahead = jnp.where(second, pltpu.roll(total, LANES - near, 1), pltpu.roll(total, LANES - far, 1))
+    behind = jnp.where(second, pltpu.roll(total, far, 1), pltpu.roll(total, near, 1))
+    partner = jnp.where(lane < HALF, ahead, behind)
+    differ = jnp.where(second == (lane < HALF), differ, -differ)
     out = weight * (both * total + differ * partner)
     out_ref[...] = jnp.broadcast_to(out, out_ref.shape)
 
 
-def apply_kernel(atoms_ref, w_ref, energy_ref, force_ref, real_ref, imag_ref):
-    x, y, z, charges = atoms_ref[0:1, :], atoms_ref[1:2, :], atoms_ref[2:3, :], atoms_ref[3:11, :]
+def apply_kernel(atoms_ref, w_ref, energy_ref, force_ref, turned_ref):
+    x, y, z, charges = atoms_ref[8:9, :], atoms_ref[9:10, :], atoms_ref[10:11, :], atoms_ref[0:8, :]
     atoms = x.shape[1]
     cx, sx = table(x)
     cy, sy = table(y)
@@ -205,26 +223,21 @@
     sq = z_rows(sz, none, charges)
     dc = [n * sq[n] for n in range(TOP + 1)]
     ds = [-n * cq[n] for n in range(TOP + 1)]
-    blank = lambda n: [jnp.zeros((n, atoms), F32)]
-    w_hi, w_lo = split(w_ref[...].reshape(2 * TILES * ROWS, LANES))
-    first, last = slice(0, 256), slice(128, 384)
-    beside = lambda one, two: split(jnp.concatenate([stack(*one), stack(*two)], axis=1))
-    real_ref[...] = product(
-        nn, (w_hi[:, first], w_lo[:, first]), beside((cq, sq, blank(80)), (dc, ds, blank(80)))
-    )
-    imag_ref[...] = product(
-        nn,
-        (w_hi[:, last], w_lo[:, last]),
-        beside((blank(48), sq, cq, blank(32)), (blank(48), ds, dc, blank(32))),
-    )
+    blank = [jnp.zeros((256 - HALF, atoms), F32)]
+    high, low = split(jnp.concatenate([stack(cq, sq, blank), stack(dc, ds, blank)], axis=1))
+    w = w_ref[...].reshape(2 * TILES * ROWS, LANES)
+    w = jnp.concatenate([w[:, 0:256], pltpu.roll(w[:, 128:384], 256 - (HALF - 128), 1)], axis=0)
+    w_high, w_low = split(w)
+    turned_ref[...] = nn(jnp.concatenate([w_high, w_low, w_high], axis=1), jnp.concatenate([high, high, low], axis=0))
     zero = jnp.zeros((8, atoms), F32)
     sums = {"e": zero, "z": zero, "x": zero, "y": zero, "x_row": zero, "y_row": zero}
 
     def add(core, tile, re, im):
-        rows = slice(8 * (core * TILES + tile), 8 * (core * TILES + tile) + 8)
-        g, h = real_ref[rows, 0:atoms], imag_ref[rows, 0:atoms]
+        at = 8 * (core * TILES + tile)
+        real, imag = slice(at, at + 8), slice(at + 2 * TILES * ROWS, at + 2 * TILES * ROWS + 8)
+        g, h = turned_ref[real, 0:atoms], turned_ref[imag, 0:atoms]
         sums["e"] += re * g + im * h
-        sums["z"] += re * real_ref[rows, atoms : 2 * atoms] + im * imag_ref[rows, atoms : 2 * atoms]
+        sums["z"] += re * turned_ref[real, atoms : 2 * atoms] + im * turned_ref[imag, atoms : 2 * atoms]
         return im * g - re * h
 
     for tile in range(13):
@@ -274,20 +287,22 @@
     copies = lax.axis_size("zh")
     shape = lambda *s: jax.ShapeDtypeStruct(s, F32)
     core = lax.axis_index("c").astype(jnp.int32).reshape(1)
-    tile = lax.axis_index(("y", "x")).astype(jnp.int32).reshape(1)
+    from_root = [(lax.axis_index(axis).astype(jnp.int32) + (4 - at)) % 4 for axis, at in zip(("y", "x"), ROOT)]
+    tile = (from_root[0] * 4 + from_root[1]).reshape(1)
     place = core * (TILES * ROWS) + tile * ROWS
-    own = jnp.concatenate([positions, charges], axis=0)
+    own = jnp.concatenate([charges, positions, miller.astype(F32)], axis=0)
     pair = lax.all_gather(own, "c")
-    half = [pltpu.VMEM((TILES * ROWS, 2 * atoms), BF16)] * 4
-    part = call(struct_kernel, shape(TILES, ROWS, LANES), 1, half, scalar=True)(core, pair)
-    part = lax.all_to_all(part, ("y", "x"), 0, 0, tiled=True)
-    part = call(collect_kernel, shape(column, 1, USED * LANES), 2, scalar=True)(place, part, miller)
+    half = [pltpu.VMEM((2 * TILES * ROWS, 6 * atoms), BF16)]
+    sums = (shape(TILES, ROWS, LANES), shape(ROWS, 128))
+    part, counts = call(struct_kernel, sums, 1, half, scalar=True)(place, pair)
+    part = lax.all_to_all(part, AXES, 0, 0, axis_index_groups=plane_groups(), tiled=True)
+    part = call(collect_kernel, shape(column, 1, USED * LANES), 2)(part, counts)
     part = lax.all_to_all(part, AXES, 0, 0, axis_index_groups=column_groups(), tiled=True)
     weigh = functools.partial(weigh_kernel, scale, copies)
     w = call(weigh, shape(TILES, ROWS, LANES), 1, scalar=True)(tile, part)
-    w = lax.all_to_all(w, ("y", "x"), 0, 0, tiled=True)
+    w = lax.all_to_all(w, AXES, 0, 0, axis_index_groups=plane_groups(), tiled=True)
     w = lax.all_gather(w, "c")
-    wide = [pltpu.VMEM((2 * TILES * ROWS, 2 * atoms), F32)] * 2
+    wide = [pltpu.VMEM((4 * TILES * ROWS, 2 * atoms), F32)]
     energy, force = call(apply_kernel, (shape(1, atoms), shape(3, atoms)), 2, wide)(own, w)
     return energy.reshape(atoms), force
 

time: 63.1 us -> 59.1 us (0.937)
  blocking collectives: 45.6 us -> 53.5 us
  waiting for transfers between devices: 7.68 us -> 0 us
  starting transfers between devices: 3.52 us -> 0 us
  local copies, waits for them, and re-layouts: 0.01 us -> 1.37 us
  Pallas kernels: 4.41 us -> 3.22 us
  other arithmetic: 0.73 us -> 0.01 us
    all_to_all x1 -> x0, waiting for transfers between devices: 7.68 us -> none  [per_device(): part = lax.all_to_all(part, ('y', 'x'), 0, 0, tiled=True)]
    all_to_all x1 -> x2, blocking collectives: 12.4 us -> 19.1 us  [the longest x1 9.84 us: per_device(): lax.all_to_all(part, AXES, 0, 0, axis_index_groups=plane_groups(), tiled=...]
    all_to_all x1 -> x0, starting transfers between devices: 3.52 us -> none  [per_device(): part = lax.all_to_all(part, ('y', 'x'), 0, 0, tiled=True)]
    all_to_all x1, blocking collectives: 19.7 us -> 21.3 us  [per_device(): lax.all_to_all(part, AXES, 0, 0, axis_index_groups=column_groups(), tiled...]
    unnamed x2 -> x6, local copies, waits for them, and re-layouts: 0.01 us -> 1.37 us
    pallas_call x2, Pallas kernels: 2.18 us -> 1.11 us  [the longest x1 1.03 us: per_device(): part, counts = call(struct_kernel, sums, 1, half, scalar=True)(place, pair)]
    unnamed x1, other arithmetic: 0.73 us -> 0.01 us
  transfers between devices with their start and end apart: 1 -> 0, of which waited for: 1 -> 0; matrix products, arithmetic and copies ran while one was open for 0% -> 0% of each run, Pallas kernels for 0% -> 0%
where the time goes in v3:
time: 59.1 us; the launch traced here: 58.8 us
  blocking collectives  53.5 us (91%)
  Pallas kernels  3.22 us (5%)
  local copies, waits for them, and re-layouts  1.37 us (2%)
  between operations  0.7 us (1%)
    all_to_all x1, blocking collectives, per_device(): lax.all_to_all(part, AXES, 0, 0, axis_index_groups=column_groups(), tiled...  21.3 us
    all_to_all x1, blocking collectives, per_device(): lax.all_to_all(part, AXES, 0, 0, axis_index_groups=plane_groups(), tiled=...  9.84 us
    all_to_all x1, blocking collectives, per_device(): lax.all_to_all(w, AXES, 0, 0, axis_index_groups=plane_groups(), tiled=True)  9.24 us
    all_gather x1, blocking collectives, per_device(): pair = lax.all_gather(own, 'c')  8.38 us
    all_gather x1, blocking collectives, per_device(): w = lax.all_gather(w, 'c')  4.73 us
    pallas_call x1, Pallas kernels, per_device(): call(apply_kernel, (shape(1, atoms), shape(3, atoms)), 2, wide)(own, w)  1.86 us
    unnamed x6, local copies, waits for them, and re-layouts  1.37 us

profile of v3, /device:TPU:1, one launch (start us, length us, event | category | flops | bytes accessed | tf_op | source)
XLA Modules:
  0.0 58.8 jit_solution(16129681037374118269)
XLA Ops:
  0.6 0.0 copy-start.2
  0.7 0.0 copy-start
  0.7 0.7 %copy-done.2 = s32[3,512]{1,0:T(4,128)S(1)} copy-done((s32[3,512]{1,0:T(4,128)S(1)}, s32[3,512]{1,0:T(4,128)}, u32[]{:S(2)}) %copy-start.2) | copy-done | bytes 6168
  1.3 0.0 copy-start.1
  1.3 0.0 copy-done
  1.4 0.7 %copy-done.1 = f32[3,512]{1,0:T(4,128)S(1)} copy-done((f32[3,512]{1,0:T(4,128)S(1)}, f32[3,512]{1,0:T(4,128)}, u32[]{:S(2)}) %copy-start.1) | copy-done | bytes 6168
  2.1 8.4 %all-gather.2.atoms_ref = f32[2,14,512]{2,1,0:T(8,128)S(1)} all-gather(f32[1,14,512]{2,1,0:T(8,128)S(1)} %get-tuple-element.10), channel_id=2, replica_groups=mesh['zl'=8,'y'=4,'zh'=2,'x'=4,'c'=2] {'c'}, dimensions={0}, use_global_device_ids=true | all-gather | bytes 86016 | tf_op jit(solution)/shard_map/all_gather | solution.py:294
  10.4 1.0 %shard_map.50 = (f32[16,8,384]{2,1,0:T(8,128)S(1)}, f32[8,128]{1,0:T(8,128)S(1)}) custom-call(s32[1]{0:T(128)S(6)} %add.24.place_ref, f32[2,14,512]{2,1,0:T(8,128)S(1)} %all-gather.2.atoms_ref), custom_call_target="tpu_custom_call" | custom-call | tf_op jit(solution)/shard_map/pallas_call | solution.py:297
  11.5 9.8 %all_to_all.15.part_ref = f32[16,8,384]{2,1,0:T(8,128)S(1)} all-to-all(f32[16,8,384]{2,1,0:T(8,128)S(1)} %get-tuple-element.6), channel_id=1, replica_groups={{36,38,32,34,52,54,48,50,4,6,0,2,20,22,16,18},{37,39,33,35,53,55,49,51,..., dimensions={0} | all-to-all | bytes 393216 | tf_op jit(solution)/shard_map/all_to_all | solution.py:298
  21.3 0.1 shard_map.51
  21.4 21.3 %all_to_all.16.part_ref = f32[16,1,2688]{2,1,0:T(1,128)S(1)} all-to-all(f32[16,1,2688]{2,1,0:T(1,128)S(1)} %shard_map.51), channel_id=1, replica_groups={{8,0,72,64,136,128,200,192,264,256,328,320,392,384,456,448},{9,1,73,65,..., dimensions={0} | all-to-all | bytes 344064 | tf_op jit(solution)/shard_map/all_to_all | solution.py:300
  42.7 0.3 shard_map.52
  42.9 9.2 %all_to_all.17 = f32[16,8,384]{2,1,0:T(8,128)S(1)} all-to-all(f32[16,8,384]{2,1,0:T(8,128)S(1)} %shard_map.52), channel_id=1, replica_groups={{36,38,32,34,52,54,48,50,4,6,0,2,20,22,16,18},{37,39,33,35,53,55,49,51,..., dimensions={0} | all-to-all | bytes 393216 | tf_op jit(solution)/shard_map/all_to_all | solution.py:303
  52.2 4.7 %all-gather.1 = f32[32,8,384]{2,1,0:T(8,128)S(1)} all-gather(f32[16,8,384]{2,1,0:T(8,128)S(1)} %all_to_all.17), channel_id=3, replica_groups=mesh['zl'=8,'y'=4,'zh'=2,'x'=4,'c'=2] {'c'}, dimensions={0}, use_global_device_ids=true | all-gather | bytes 589824 | tf_op jit(solution)/shard_map/all_gather | solution.py:304
  56.9 1.9 %shard_map.53 = (f32[1,512]{1,0:T(1,128)}, f32[3,512]{1,0:T(4,128)}) custom-call(f32[14,512]{1,0:T(8,128)S(1)} %get-tuple-element.11.atoms_ref, f32[2,16,8,384]{3,2,1,0:T(8,128)S(1)} %bitcast.6), custom_call_target="tpu_custom_call" | custom-call | tf_op jit(solution)/shard_map/pallas_call | solution.py:306
  (2 shorter events, 0.0 us)
Async XLA Ops:
  0.6 0.7 %copy-start.2 = (s32[3,512]{1,0:T(4,128)S(1)}, s32[3,512]{1,0:T(4,128)}, u32[]{:S(2)}) copy-start(s32[3,512]{1,0:T(4,128)} %param.5) | copy-start | bytes 18436
  0.7 0.7 %copy-start = (f32[8,512]{1,0:T(8,128)S(1)}, f32[8,512]{1,0:T(8,128)}, u32[]{:S(2)}) copy-start(f32[8,512]{1,0:T(8,128)} %param.4) | copy-start | bytes 49156
  1.3 0.7 %copy-start.1 = (f32[3,512]{1,0:T(4,128)S(1)}, f32[3,512]{1,0:T(4,128)}, u32[]{:S(2)}) copy-start(f32[3,512]{1,0:T(4,128)} %param.3) | copy-start | bytes 18436

commit v4 on v3

--- a/solution.py
+++ b/solution.py
@@ -12,7 +12,8 @@
 TOP = 10
 TILES = 16
 ROWS = 8
-USED = 7
+HALVES = 2 * TILES
+SHARD = 4
 HALF = 176
 LANES = 384
 COUNT_LANE = 352
@@ -32,17 +33,19 @@
 ROOT = (2, 2)
 
 
+def device(z, y, x, c):
+    return int(np.arange(512).reshape(SHAPE)[z % 8, y, z // 8, x, c])
+
+
+def layer_groups():
+    chips = [((n // 4 + ROOT[0]) % 4, (n % 4 + ROOT[1]) % 4) for n in range(TILES)]
+    return [[device(z + half, y, x, c) for y, x in chips for half in (0, 1)] for z in range(0, 16, 2) for c in (0, 1)]
+
+
 def column_groups():
-    ids = np.arange(512).reshape(SHAPE)
-    order = [(8 + n // 2 + 8 * (n % 2)) % 16 for n in range(16)]
-    return [[int(ids[z % 8, y, z // 8, x, c]) for z in order] for y in range(4) for x in range(4) for c in range(2)]
-
-
-def plane_groups():
-    ids = np.arange(512).reshape(SHAPE)
-    order = [((n // 4 + ROOT[0]) % 4, (n % 4 + ROOT[1]) % 4) for n in range(16)]
-    rest = [(zl, zh, c) for zl in range(8) for zh in range(2) for c in range(2)]
-    return [[int(ids[zl, y, zh, x, c]) for y, x in order] for zl, zh, c in rest]
+    order = [(8 + n // 2 * 2 + 8 * (n % 2)) % 16 for n in range(8)]
+    rest = [(half, y, x, c) for half in (0, 1) for y in range(4) for x in range(4) for c in (0, 1)]
+    return [[device(z + half, y, x, c) for z in order] for half, y, x, c in rest]
 
 
 def horner(coefs, u):
@@ -102,11 +105,8 @@
     return jnp.concatenate([p for part in parts for p in part], axis=0)
 
 
-def struct_kernel(place_ref, atoms_ref, out_ref, counts_ref, pairs_ref):
-    place = place_ref[0]
-    core = jnp.where(place < TILES * ROWS, 0, 1)
-    listed = [atoms_ref[0, r : r + 1, :].astype(jnp.int32) for r in (11, 12, 13)]
-    counts_ref[...] = count_listed(place, *listed)
+def struct_kernel(where_ref, atoms_ref, out_ref, pairs_ref):
+    core, mine = where_ref[0] // HALVES, where_ref[0] % HALVES // 2
     both = jnp.concatenate([atoms_ref[0], atoms_ref[1]], axis=1)
     lanes = both.shape[1]
     x, z, charges = both[8:9], both[10:11], both[0:8]
@@ -141,9 +141,17 @@
     high, low = split(stack(cq, sq, [jnp.zeros((256 - HALF, lanes), F32)]))
     sums = nt(pairs_ref[...], jnp.concatenate([high, high, low], axis=1))
     real, imag = sums[0:128], pltpu.roll(sums[128:256], HALF - 128, 1)
-    out_ref[:, :, 0:128] = real[:, 0:128].reshape(TILES, ROWS, 128)
-    out_ref[:, :, 128:256] = (real[:, 128:256] + imag[:, 0:128]).reshape(TILES, ROWS, 128)
-    out_ref[:, :, 256:384] = imag[:, 128:256].reshape(TILES, ROWS, 128)
+    middle = real[:, 128:256] + imag[:, 0:128]
+    for n in range(HALVES):
+        rows = slice(SHARD * n, SHARD * n + SHARD)
+        out_ref[n, :, 0:128] = real[rows, 0:128]
+        out_ref[n, :, 128:256] = middle[rows]
+        out_ref[n, :, 256:384] = imag[rows, 128:256]
+    listed = [atoms_ref[0, r : r + 1, :].astype(jnp.int32) for r in (11, 12, 13)]
+    counts = count_listed((core * TILES + mine) * ROWS, *listed)
+    for half in range(2):
+        own = out_ref.at[2 * mine + half, :, 256:384]
+        own[...] = own[...] + counts[SHARD * half : SHARD * half + SHARD]
 
 
 def place_of(a, b):
@@ -167,20 +175,14 @@
     return nt(pair.astype(BF16), third.astype(BF16))
 
 
-def collect_kernel(part_ref, counts_ref, out_ref):
-    total = jnp.sum(part_ref[...], axis=0)
-    copies = out_ref.shape[0]
-    for r in range(USED):
-        out_ref[:, :, LANES * r : LANES * r + 256] = jnp.broadcast_to(total[r : r + 1, 0:256], (copies, 1, 256))
-        last = total[r : r + 1, 256:384] + counts_ref[r : r + 1, :]
-        out_ref[:, :, LANES * r + 256 : LANES * r + 384] = jnp.broadcast_to(last, (copies, 1, 128))
-
-
-def weigh_kernel(scale, copies, tile_ref, part_ref, out_ref):
-    flat = jnp.sum(part_ref[...], axis=0)
-    total = stack([flat[:, LANES * r : LANES * r + LANES] for r in range(USED)], [jnp.zeros((1, LANES), F32)])
-    tile = tile_ref[0]
-    row = lax.broadcasted_iota(jnp.int32, (ROWS, LANES), 0)
+def collect_kernel(part_ref, out_ref):
+    out_ref[...] = jnp.broadcast_to(jnp.sum(part_ref[...], axis=0), out_ref.shape)
+
+
+def weigh_kernel(scale, copies, where_ref, part_ref, out_ref):
+    total = stack([jnp.sum(part_ref[...], axis=0), jnp.zeros((ROWS - SHARD, LANES), F32)])
+    tile = where_ref[0] % HALVES // 2
+    row = lax.broadcasted_iota(jnp.int32, (ROWS, LANES), 0) + SHARD * (where_ref[0] % 2)
     lane = lax.broadcasted_iota(jnp.int32, (ROWS, LANES), 1)
     inner = jnp.where(lane >= HALF, lane - HALF, lane)
     second = inner >= HALF // 2
@@ -209,7 +211,7 @@
     partner = jnp.where(lane < HALF, ahead, behind)
     differ = jnp.where(second == (lane < HALF), differ, -differ)
     out = weight * (both * total + differ * partner)
-    out_ref[...] = jnp.broadcast_to(out, out_ref.shape)
+    out_ref[...] = jnp.broadcast_to(out[0:SHARD], out_ref.shape)
 
 
 def apply_kernel(atoms_ref, w_ref, energy_ref, force_ref, turned_ref):
@@ -225,7 +227,7 @@
     ds = [-n * cq[n] for n in range(TOP + 1)]
     blank = [jnp.zeros((256 - HALF, atoms), F32)]
     high, low = split(jnp.concatenate([stack(cq, sq, blank), stack(dc, ds, blank)], axis=1))
-    w = w_ref[...].reshape(2 * TILES * ROWS, LANES)
+    w = stack([w_ref[core, n] for core in range(2) for n in range(HALVES)])
     w = jnp.concatenate([w[:, 0:256], pltpu.roll(w[:, 128:384], 256 - (HALF - 128), 1)], axis=0)
     w_high, w_low = split(w)
     turned_ref[...] = nn(jnp.concatenate([w_high, w_low, w_high], axis=1), jnp.concatenate([high, high, low], axis=0))
@@ -283,24 +285,24 @@
 
 def per_device(scale, positions, charges, miller):
     atoms = positions.shape[1]
-    column = lax.axis_size("zl") * lax.axis_size("zh")
     copies = lax.axis_size("zh")
     shape = lambda *s: jax.ShapeDtypeStruct(s, F32)
     core = lax.axis_index("c").astype(jnp.int32).reshape(1)
     from_root = [(lax.axis_index(axis).astype(jnp.int32) + (4 - at)) % 4 for axis, at in zip(("y", "x"), ROOT)]
     tile = (from_root[0] * 4 + from_root[1]).reshape(1)
-    place = core * (TILES * ROWS) + tile * ROWS
-    own = jnp.concatenate([charges, positions, miller.astype(F32)], axis=0)
+    where = core * HALVES + tile * 2 + (lax.axis_index("zl").astype(jnp.int32) & 1)
+    rows = lambda a, first: jnp.pad(a, ((first, 16 - first - a.shape[0]), (0, 0)))
+    own = rows(charges, 0) + rows(positions, 8) + rows(miller, 11).astype(F32)
     pair = lax.all_gather(own, "c")
     half = [pltpu.VMEM((2 * TILES * ROWS, 6 * atoms), BF16)]
-    sums = (shape(TILES, ROWS, LANES), shape(ROWS, 128))
-    part, counts = call(struct_kernel, sums, 1, half, scalar=True)(place, pair)
-    part = lax.all_to_all(part, AXES, 0, 0, axis_index_groups=plane_groups(), tiled=True)
-    part = call(collect_kernel, shape(column, 1, USED * LANES), 2)(part, counts)
-    part = lax.all_to_all(part, AXES, 0, 0, axis_index_groups=column_groups(), tiled=True)
+    layer, column = layer_groups(), column_groups()
+    part = call(struct_kernel, shape(HALVES, SHARD, LANES), 1, half, scalar=True)(where, pair)
+    part = lax.all_to_all(part, AXES, 0, 0, axis_index_groups=layer, tiled=True)
+    part = call(collect_kernel, shape(len(column[0]), SHARD, LANES), 1)(part)
+    part = lax.all_to_all(part, AXES, 0, 0, axis_index_groups=column, tiled=True)
     weigh = functools.partial(weigh_kernel, scale, copies)
-    w = call(weigh, shape(TILES, ROWS, LANES), 1, scalar=True)(tile, part)
-    w = lax.all_to_all(w, AXES, 0, 0, axis_index_groups=plane_groups(), tiled=True)
+    w = call(weigh, shape(HALVES, SHARD, LANES), 1, scalar=True)(where, part)
+    w = lax.all_to_all(w, AXES, 0, 0, axis_index_groups=layer, tiled=True)
     w = lax.all_gather(w, "c")
     wide = [pltpu.VMEM((4 * TILES * ROWS, 2 * atoms), F32)]
     energy, force = call(apply_kernel, (shape(1, atoms), shape(3, atoms)), 2, wide)(own, w)

time: 59.1 us -> 57.1 us (0.966)
  blocking collectives: 53.5 us -> 52.2 us
  local copies, waits for them, and re-layouts: 1.37 us -> 0.69 us
    all_to_all x3, blocking collectives: 40.3 us -> 38.1 us  [the longest x1 17 us: per_device(): lax.all_to_all(part, AXES, 0, 0, axis_index_groups=column, tiled=True)]
    all_gather x1, blocking collectives: 4.73 us -> 5.72 us  [per_device(): w = lax.all_gather(w, 'c')]
    unnamed x6, local copies, waits for them, and re-layouts: 1.37 us -> 0.69 us
where the time goes in v4:
time: 57.1 us; the launch traced here: 56.7 us
  blocking collectives  52.2 us (91%)
  Pallas kernels  3.12 us (5%)
  between operations  0.7 us (1%)
  local copies, waits for them, and re-layouts  0.69 us (1%)
    all_to_all x1, blocking collectives, per_device(): lax.all_to_all(part, AXES, 0, 0, axis_index_groups=column, tiled=True)  17 us
    all_to_all x1, blocking collectives, per_device(): w = lax.all_to_all(w, AXES, 0, 0, axis_index_groups=layer, tiled=True)  10.9 us
    all_to_all x1, blocking collectives, per_device(): part = lax.all_to_all(part, AXES, 0, 0, axis_index_groups=layer, tiled=True)  10.2 us
    all_gather x1, blocking collectives, per_device(): pair = lax.all_gather(own, 'c')  8.38 us
    all_gather x1, blocking collectives, per_device(): w = lax.all_gather(w, 'c')  5.72 us
    pallas_call x1, Pallas kernels, per_device(): call(apply_kernel, (shape(1, atoms), shape(3, atoms)), 2, wide)(own, w)  1.86 us

profile of v4, /device:TPU:1, one launch (start us, length us, event | category | flops | bytes accessed | tf_op | source)
XLA Modules:
  0.0 56.7 jit_solution(13468117615900582846)
XLA Ops:
  0.6 0.0 copy-start
  0.7 0.0 copy-start.2
  0.7 0.0 copy-start.1
  0.7 0.7 %copy-done = f32[8,512]{1,0:T(8,128)S(1)} copy-done((f32[8,512]{1,0:T(8,128)S(1)}, f32[8,512]{1,0:T(8,128)}, u32[]{:S(2)}) %copy-start) | copy-done | bytes 16408
  1.4 0.0 copy-done.2
  1.4 0.0 copy-done.1
  1.4 8.4 %all-gather = f32[32,512]{1,0:T(8,128)S(1)} all-gather(f32[16,512]{1,0:T(8,128)S(1)} %convert_add_fusion.atoms_ref), channel_id=2, replica_groups=mesh['zl'=8,'y'=4,'zh'=2,'x'=4,'c'=2] {'c'}, dimensions={0}, use_global_device_ids=true | all-gather | bytes 98304 | tf_op jit(solution)/shard_map/all_gather | solution.py:296
  9.8 1.0 %shard_map.50 = f32[32,4,384]{2,1,0:T(4,128)S(1)} custom-call(s32[1]{0:T(128)} %bitcast.where_ref, f32[2,16,512]{2,1,0:T(8,128)S(1)} %bitcast.5), custom_call_target="tpu_custom_call" | custom-call | tf_op jit(solution)/shard_map/pallas_call | solution.py:299
  10.8 10.2 %all_to_all.15.part_ref = f32[32,4,384]{2,1,0:T(4,128)S(1)} all-to-all(f32[32,4,384]{2,1,0:T(4,128)S(1)} %shard_map.50), channel_id=1, replica_groups={{36,100,38,102,32,96,34,98,52,116,54,118,48,112,50,114,4,68,6,70,0,64,2..., dimensions={0} | all-to-all | bytes 393216 | tf_op jit(solution)/shard_map/all_to_all | solution.py:300
  21.0 0.1 shard_map.51
  21.0 17.0 %all_to_all.16.part_ref = f32[8,4,384]{2,1,0:T(4,128)S(1)} all-to-all(f32[8,4,384]{2,1,0:T(4,128)S(1)} %shard_map.51), channel_id=1, replica_groups={{8,0,136,128,264,256,392,384},{9,1,137,129,265,257,393,385},{10,2,138,1..., dimensions={0} | all-to-all | bytes 98304 | tf_op jit(solution)/shard_map/all_to_all | solution.py:302
  38.0 0.2 shard_map.52
  38.2 10.9 %all_to_all.17 = f32[32,4,384]{2,1,0:T(4,128)S(1)} all-to-all(f32[32,4,384]{2,1,0:T(4,128)S(1)} %shard_map.52), channel_id=1, replica_groups={{36,100,38,102,32,96,34,98,52,116,54,118,48,112,50,114,4,68,6,70,0,64,2..., dimensions={0} | all-to-all | bytes 393216 | tf_op jit(solution)/shard_map/all_to_all | solution.py:305
  49.1 5.7 %all-gather.1 = f32[64,4,384]{2,1,0:T(4,128)S(1)} all-gather(f32[32,4,384]{2,1,0:T(4,128)S(1)} %all_to_all.17), channel_id=3, replica_groups=mesh['zl'=8,'y'=4,'zh'=2,'x'=4,'c'=2] {'c'}, dimensions={0}, use_global_device_ids=true | all-gather | bytes 589824 | tf_op jit(solution)/shard_map/all_gather | solution.py:306
  54.8 1.9 %shard_map.53 = (f32[1,512]{1,0:T(1,128)}, f32[3,512]{1,0:T(4,128)}) custom-call(f32[16,512]{1,0:T(8,128)S(1)} %convert_add_fusion.atoms_ref, f32[2,32,4,384]{3,2,1,0:T(4,128)S(1)} %bitcast.4), custom_call_target="tpu_custom_call" | custom-call | tf_op jit(solution)/shard_map/pallas_call | solution.py:308
  (1 shorter events, 0.0 us)
Async XLA Ops:
  0.6 0.7 %copy-start = (f32[8,512]{1,0:T(8,128)S(1)}, f32[8,512]{1,0:T(8,128)}, u32[]{:S(2)}) copy-start(f32[8,512]{1,0:T(8,128)} %param.4) | copy-start | bytes 49156
  0.7 0.7 %copy-start.2 = (f32[3,512]{1,0:T(4,128)S(1)}, f32[3,512]{1,0:T(4,128)}, u32[]{:S(2)}) copy-start(f32[3,512]{1,0:T(4,128)} %param.3) | copy-start | bytes 18436
  0.7 0.7 %copy-start.1 = (s32[3,512]{1,0:T(4,128)S(1)}, s32[3,512]{1,0:T(4,128)}, u32[]{:S(2)}) copy-start(s32[3,512]{1,0:T(4,128)} %param.5) | copy-start | bytes 18436

commit v5 on v4

--- a/solution.py
+++ b/solution.py
@@ -39,7 +39,7 @@
 
 def layer_groups():
     chips = [((n // 4 + ROOT[0]) % 4, (n % 4 + ROOT[1]) % 4) for n in range(TILES)]
-    return [[device(z + half, y, x, c) for y, x in chips for half in (0, 1)] for z in range(0, 16, 2) for c in (0, 1)]
+    return [[device(z + half, y, x, c) for half in (1, 0) for y, x in chips] for z in range(0, 16, 2) for c in (0, 1)]
 
 
 def column_groups():
@@ -62,17 +62,14 @@
     return 1.0 - 2.0 * s * s, 2.0 * s * horner(COS, u)
 
 
-def table(coordinate):
+def late_orders(row, steps):
+    third = jnp.where(row >= 6, 2, jnp.where(row >= 3, 1, 0))
+    return 8 + (third if steps else row - 3 * third)
+
+
+def table(coordinate, steps=False):
     r = lax.broadcasted_iota(jnp.int32, (16, coordinate.shape[1]), 0)
-    return cos_sin(jnp.where(r < TOP, r + 1, 0).astype(F32) * coordinate)
-
-
-def late_orders(core, lanes):
-    q = lax.broadcasted_iota(jnp.int32, (24, lanes), 0)
-    n = jnp.where(q < 7, q, jnp.where((q >= 8) & (q < 12), q - 1, 0))
-    late_a = jnp.where((q >= 12) & (q < 15), 8, jnp.where((q >= 16) & (q < 19), 9, jnp.where((q >= 19) & (q < 22), 10, 0)))
-    late_b = jnp.where(late_a == 8, q - 4, jnp.where(late_a == 9, q - 8, jnp.where(late_a == 10, q - 11, 0)))
-    return jnp.where(core == 0, n + late_a, late_a).astype(F32), jnp.where(core == 0, late_b, n + late_b).astype(F32)
+    return cos_sin(jnp.where(r < 8, r, late_orders(r - 8, steps)).astype(F32) * coordinate)
 
 
 def split(x):
@@ -81,16 +78,24 @@
 
 
 def factors(tile, cx, sx, cy, sy):
-    if tile < 10:
-        ca, sa, cb, sb = cx[0:8], sx[0:8], cy[tile : tile + 1], sy[tile : tile + 1]
+    if tile < 11:
+        b = (tile + 1) % 11
+        rows, at = slice(0, 8), b if b < 8 else 3 * b - 16
+        columns = slice(at, at + 1)
+    elif tile < 14:
+        rows, columns = slice(tile - 3, tile - 2), slice(0, 8)
+    elif tile == 14:
+        rows, columns = slice(8, 16), slice(8, 16)
     else:
-        r = tile - 3
-        ca, sa, cb, sb = cx[r : r + 1], sx[r : r + 1], cy[0:8], sy[0:8]
+        rows, columns = slice(10, 11), slice(14, 15)
+    ca, sa, cb, sb = cx[rows], sx[rows], cy[columns], sy[columns]
+    if tile == 15:
+        ca, sa = jnp.broadcast_to(ca, (8, ca.shape[1])), jnp.broadcast_to(sa, (8, sa.shape[1]))
     return ca * cb, sa * sb, sa * cb, ca * sb
 
 
-def z_rows(rows, first, charges):
-    return [first] + [rows[n : n + 1] * charges for n in range(TOP)]
+def z_rows(rows, charges):
+    return [rows[n : n + 1] * charges for n in range(TOP + 1)]
 
 
 def nt(a, b):
@@ -112,10 +117,8 @@
     x, z, charges = both[8:9], both[10:11], both[0:8]
     y = both[9:10] * jnp.where(core == 0, 1.0, -1.0)
     cx, sx = table(x)
-    cy, sy = table(y)
+    cy, sy = table(y, steps=True)
     cz, sz = table(z)
-    a, b = late_orders(core, lanes)
-    late_c, late_s = cos_sin(a * x + b * y)
 
     def keep(rows, value):
         high, low = split(value)
@@ -126,42 +129,36 @@
     for two in range(TILES // 2):
         real, imag = [], []
         for tile in (2 * two, 2 * two + 1):
-            if tile < 13:
-                cc, ss, sc, cs = factors(tile, cx, sx, cy, sy)
-                real.append(cc - ss)
-                imag.append(sc + cs)
-            else:
-                rows = slice(8 * (tile - 13), 8 * (tile - 12))
-                real.append(late_c[rows])
-                imag.append(late_s[rows])
+            cc, ss, sc, cs = factors(tile, cx, sx, cy, sy)
+            real.append(cc - ss)
+            imag.append(sc + cs)
         keep(slice(16 * two, 16 * two + 16), stack(real))
         keep(slice(128 + 16 * two, 128 + 16 * two + 16), stack(imag))
-    cq = z_rows(cz, charges, charges)
-    sq = z_rows(sz, jnp.zeros_like(charges), charges)
+    cq = z_rows(cz, charges)
+    sq = z_rows(sz, charges)
     high, low = split(stack(cq, sq, [jnp.zeros((256 - HALF, lanes), F32)]))
     sums = nt(pairs_ref[...], jnp.concatenate([high, high, low], axis=1))
     real, imag = sums[0:128], pltpu.roll(sums[128:256], HALF - 128, 1)
     middle = real[:, 128:256] + imag[:, 0:128]
     for n in range(HALVES):
-        rows = slice(SHARD * n, SHARD * n + SHARD)
+        at = ROWS * (n % TILES) + SHARD * (n // TILES)
+        rows = slice(at, at + SHARD)
         out_ref[n, :, 0:128] = real[rows, 0:128]
         out_ref[n, :, 128:256] = middle[rows]
         out_ref[n, :, 256:384] = imag[rows, 128:256]
     listed = [atoms_ref[0, r : r + 1, :].astype(jnp.int32) for r in (11, 12, 13)]
     counts = count_listed((core * TILES + mine) * ROWS, *listed)
     for half in range(2):
-        own = out_ref.at[2 * mine + half, :, 256:384]
+        own = out_ref.at[TILES * half + mine, :, 256:384]
         own[...] = own[...] + counts[SHARD * half : SHARD * half + SHARD]
 
 
 def place_of(a, b):
     core = jnp.where(b < 0, 1, 0)
     b = jnp.abs(b)
-    n = a + b
-    axis = jnp.where(n <= 6, 13 * 8 + n, 14 * 8 + n - 7)
-    corner = jnp.where(a == 8, 14 * 8 + b - 4, 15 * 8 + (a - 9) * 3 + b - 8)
-    rest = jnp.where(a <= 7, (b - 1) * 8 + a - 1, jnp.where(b <= 7, (a + 2) * 8 + b - 1, corner))
-    return core * (TILES * ROWS) + jnp.where((a == 0) | (b == 0), axis, rest)
+    corner = 14 * 8 + a - 8 + 3 * (b - 8)
+    late = jnp.where(b <= 7, (a + 3) * 8 + b, corner)
+    return core * (TILES * ROWS) + jnp.where(a <= 7, jnp.where(b == 0, 10, b - 1) * 8 + a, late)
 
 
 def count_listed(place, a, b, c):
@@ -187,12 +184,10 @@
     inner = jnp.where(lane >= HALF, lane - HALF, lane)
     second = inner >= HALF // 2
     c = jnp.where(second, inner - HALF // 2, inner) >> 3
-    a = jnp.where(tile < 10, tile + 1, jnp.where(tile < 13, tile - 2, 0))
-    b = row + 1
-    a = jnp.where(tile == 13, 0, jnp.where(tile == 14, jnp.where(row < 4, 0, 8), a))
-    b = jnp.where(tile == 13, row, jnp.where(tile == 14, jnp.where(row < 4, row + 7, row + 4), b))
-    a = jnp.where(tile == 15, jnp.where(row < 3, 9, 10), a)
-    b = jnp.where(tile == 15, jnp.where(row < 3, row + 8, row + 5), b)
+    late = tile >= 14
+    a = jnp.where(tile < 11, row, jnp.where(late, late_orders(row, False), tile - 3))
+    b = jnp.where(tile < 10, tile + 1, jnp.where(tile == 10, 0, jnp.where(late, late_orders(row, True), row)))
+    a, b = jnp.where(tile == 15, 10, a), jnp.where(tile == 15, 10, b)
     square = jnp.maximum(a * a + b * b + c * c, 1).astype(F32)
     weight = jnp.exp(-0.025 * square) / square * scale
     wide_lane = lax.broadcasted_iota(jnp.int32, (128, LANES), 1)
@@ -218,16 +213,15 @@
     x, y, z, charges = atoms_ref[8:9, :], atoms_ref[9:10, :], atoms_ref[10:11, :], atoms_ref[0:8, :]
     atoms = x.shape[1]
     cx, sx = table(x)
-    cy, sy = table(y)
+    cy, sy = table(y, steps=True)
     cz, sz = table(z)
-    none = jnp.zeros_like(charges)
-    cq = z_rows(cz, charges, charges)
-    sq = z_rows(sz, none, charges)
+    cq = z_rows(cz, charges)
+    sq = z_rows(sz, charges)
     dc = [n * sq[n] for n in range(TOP + 1)]
     ds = [-n * cq[n] for n in range(TOP + 1)]
     blank = [jnp.zeros((256 - HALF, atoms), F32)]
     high, low = split(jnp.concatenate([stack(cq, sq, blank), stack(dc, ds, blank)], axis=1))
-    w = stack([w_ref[core, n] for core in range(2) for n in range(HALVES)])
+    w = stack([w_ref[core, n] for core in range(2) for tile in range(TILES) for n in (tile, TILES + tile)])
     w = jnp.concatenate([w[:, 0:256], pltpu.roll(w[:, 128:384], 256 - (HALF - 128), 1)], axis=0)
     w_high, w_low = split(w)
     turned_ref[...] = nn(jnp.concatenate([w_high, w_low, w_high], axis=1), jnp.concatenate([high, high, low], axis=0))
@@ -242,25 +236,22 @@
         sums["z"] += re * turned_ref[real, atoms : 2 * atoms] + im * turned_ref[imag, atoms : 2 * atoms]
         return im * g - re * h
 
-    for tile in range(13):
+    order = lax.broadcasted_iota(jnp.int32, (8, atoms), 0)
+    for tile in range(TILES):
         cc, ss, sc, cs = factors(tile, cx, sx, cy, sy)
-        up, down = add(0, tile, cc - ss, sc + cs), add(1, tile, cc + ss, sc - cs)
-        if tile < 10:
+        up = add(0, tile, cc - ss, sc + cs)
+        down = add(1, tile, cc + ss, sc - cs) if tile != 10 else jnp.zeros_like(up)
+        if tile < 11:
             sums["x_row"] += up + down
-            sums["y"] += (tile + 1.0) * (up - down)
+            sums["y"] += ((tile + 1.0) % 11.0) * (up - down)
+        elif tile < 14:
+            sums["x"] += (tile - 3.0) * (up + down)
+            sums["y_row"] += up - down
         else:
-            sums["x"] += (tile - 2.0) * (up + down)
-            sums["y_row"] += up - down
-    for core in range(2):
-        a, b = late_orders(core, atoms)
-        b = b * (1.0 - 2.0 * core)
-        late_c, late_s = cos_sin(a * x + b * y)
-        for j in range(3):
-            rows = slice(8 * j, 8 * j + 8)
-            d = add(core, 13 + j, late_c[rows], late_s[rows])
-            sums["x"] += a[rows] * d
-            sums["y"] += b[rows] * d
-    order = lax.broadcasted_iota(jnp.int32, (8, atoms), 0).astype(F32) + 1.0
+            late = [late_orders(order, steps).astype(F32) if tile == 14 else 10.0 for steps in (False, True)]
+            sums["x"] += late[0] * (up + down)
+            sums["y"] += late[1] * (up - down)
+    order = order.astype(F32)
     down = lambda v: jnp.sum(v, axis=0, keepdims=True)
     energy_ref[...] = 0.25 * down(sums["e"])
     force_ref[0:1, :] = 0.1 * down(sums["x"] + order * sums["x_row"])
@@ -290,7 +281,7 @@
     core = lax.axis_index("c").astype(jnp.int32).reshape(1)
     from_root = [(lax.axis_index(axis).astype(jnp.int32) + (4 - at)) % 4 for axis, at in zip(("y", "x"), ROOT)]
     tile = (from_root[0] * 4 + from_root[1]).reshape(1)
-    where = core * HALVES + tile * 2 + (lax.axis_index("zl").astype(jnp.int32) & 1)
+    where = core * HALVES + tile * 2 + 1 - (lax.axis_index("zl").astype(jnp.int32) & 1)
     rows = lambda a, first: jnp.pad(a, ((first, 16 - first - a.shape[0]), (0, 0)))
     own = rows(charges, 0) + rows(positions, 8) + rows(miller, 11).astype(F32)
     pair = lax.all_gather(own, "c")

time: 57.1 us -> 55.8 us (0.977)
  blocking collectives: 52.2 us -> 51 us
    all_to_all x1, blocking collectives: 17 us -> 16.3 us  [per_device(): lax.all_to_all(part, AXES, 0, 0, axis_index_groups=column, tiled=True)]
where the time goes in v5:
time: 55.8 us; the launch traced here: 55.4 us
  blocking collectives  51 us (91%)
  Pallas kernels  2.98 us (5%)
  between operations  0.7 us (1%)
  local copies, waits for them, and re-layouts  0.69 us (1%)
    all_to_all x1, blocking collectives, per_device(): lax.all_to_all(part, AXES, 0, 0, axis_index_groups=column, tiled=True)  16.3 us
    all_to_all x1, blocking collectives, per_device(): w = lax.all_to_all(w, AXES, 0, 0, axis_index_groups=layer, tiled=True)  10.9 us
    all_to_all x1, blocking collectives, per_device(): part = lax.all_to_all(part, AXES, 0, 0, axis_index_groups=layer, tiled=True)  10.2 us
    all_gather x1, blocking collectives, per_device(): pair = lax.all_gather(own, 'c')  8.38 us
    all_gather x1, blocking collectives, per_device(): w = lax.all_gather(w, 'c')  5.21 us
    pallas_call x1, Pallas kernels, per_device(): call(apply_kernel, (shape(1, atoms), shape(3, atoms)), 2, wide)(own, w)  1.79 us

profile of v5, /device:TPU:1, one launch (start us, length us, event | category | flops | bytes accessed | tf_op | source)
XLA Modules:
  0.0 55.4 jit_solution(15273767627029562069)
XLA Ops:
  0.6 0.0 copy-start
  0.7 0.0 copy-start.2
  0.7 0.0 copy-start.1
  0.7 0.7 %copy-done = f32[8,512]{1,0:T(8,128)S(1)} copy-done((f32[8,512]{1,0:T(8,128)S(1)}, f32[8,512]{1,0:T(8,128)}, u32[]{:S(2)}) %copy-start) | copy-done | bytes 16408
  1.4 0.0 copy-done.2
  1.4 0.0 copy-done.1
  1.4 8.4 %all-gather = f32[32,512]{1,0:T(8,128)S(1)} all-gather(f32[16,512]{1,0:T(8,128)S(1)} %convert_add_fusion.atoms_ref), channel_id=2, replica_groups=mesh['zl'=8,'y'=4,'zh'=2,'x'=4,'c'=2] {'c'}, dimensions={0}, use_global_device_ids=true | all-gather | bytes 98304 | tf_op jit(solution)/shard_map/all_gather | solution.py:287
  9.8 0.9 %shard_map.50 = f32[32,4,384]{2,1,0:T(4,128)S(1)} custom-call(s32[1]{0:T(128)} %bitcast.where_ref, f32[2,16,512]{2,1,0:T(8,128)S(1)} %bitcast.5), custom_call_target="tpu_custom_call" | custom-call | tf_op jit(solution)/shard_map/pallas_call | solution.py:290
  10.7 10.2 %all_to_all.15.part_ref = f32[32,4,384]{2,1,0:T(4,128)S(1)} all-to-all(f32[32,4,384]{2,1,0:T(4,128)S(1)} %shard_map.50), channel_id=1, replica_groups={{100,102,96,98,116,118,112,114,68,70,64,66,84,86,80,82,36,38,32,34,52,5..., dimensions={0} | all-to-all | bytes 393216 | tf_op jit(solution)/shard_map/all_to_all | solution.py:291
  20.9 0.1 shard_map.51
  21.0 16.3 %all_to_all.16.part_ref = f32[8,4,384]{2,1,0:T(4,128)S(1)} all-to-all(f32[8,4,384]{2,1,0:T(4,128)S(1)} %shard_map.51), channel_id=1, replica_groups={{8,0,136,128,264,256,392,384},{9,1,137,129,265,257,393,385},{10,2,138,1..., dimensions={0} | all-to-all | bytes 98304 | tf_op jit(solution)/shard_map/all_to_all | solution.py:293
  37.3 0.2 shard_map.52
  37.5 10.9 %all_to_all.17 = f32[32,4,384]{2,1,0:T(4,128)S(1)} all-to-all(f32[32,4,384]{2,1,0:T(4,128)S(1)} %shard_map.52), channel_id=1, replica_groups={{100,102,96,98,116,118,112,114,68,70,64,66,84,86,80,82,36,38,32,34,52,5..., dimensions={0} | all-to-all | bytes 393216 | tf_op jit(solution)/shard_map/all_to_all | solution.py:296
  48.4 5.2 %all-gather.1 = f32[64,4,384]{2,1,0:T(4,128)S(1)} all-gather(f32[32,4,384]{2,1,0:T(4,128)S(1)} %all_to_all.17), channel_id=3, replica_groups=mesh['zl'=8,'y'=4,'zh'=2,'x'=4,'c'=2] {'c'}, dimensions={0}, use_global_device_ids=true | all-gather | bytes 589824 | tf_op jit(solution)/shard_map/all_gather | solution.py:297
  53.6 1.8 %shard_map.53 = (f32[1,512]{1,0:T(1,128)}, f32[3,512]{1,0:T(4,128)}) custom-call(f32[16,512]{1,0:T(8,128)S(1)} %convert_add_fusion.atoms_ref, f32[2,32,4,384]{3,2,1,0:T(4,128)S(1)} %bitcast.4), custom_call_target="tpu_custom_call" | custom-call | tf_op jit(solution)/shard_map/pallas_call | solution.py:299
  (1 shorter events, 0.0 us)
Async XLA Ops:
  0.6 0.7 %copy-start = (f32[8,512]{1,0:T(8,128)S(1)}, f32[8,512]{1,0:T(8,128)}, u32[]{:S(2)}) copy-start(f32[8,512]{1,0:T(8,128)} %param.4) | copy-start | bytes 49156
  0.7 0.7 %copy-start.2 = (f32[3,512]{1,0:T(4,128)S(1)}, f32[3,512]{1,0:T(4,128)}, u32[]{:S(2)}) copy-start(f32[3,512]{1,0:T(4,128)} %param.3) | copy-start | bytes 18436
  0.7 0.7 %copy-start.1 = (s32[3,512]{1,0:T(4,128)S(1)}, s32[3,512]{1,0:T(4,128)}, u32[]{:S(2)}) copy-start(s32[3,512]{1,0:T(4,128)} %param.5) | copy-start | bytes 18436

commit v6 on v5

--- a/solution.py
+++ b/solution.py
@@ -33,19 +33,20 @@
 ROOT = (2, 2)
 
 
-def device(z, y, x, c):
-    return int(np.arange(512).reshape(SHAPE)[z % 8, y, z // 8, x, c])
+def device(z, y, x, part):
+    z = z % 16
+    return int(np.arange(512).reshape(SHAPE)[z % 8, y, z // 8, x, part ^ (z // 8)])
 
 
 def layer_groups():
     chips = [((n // 4 + ROOT[0]) % 4, (n % 4 + ROOT[1]) % 4) for n in range(TILES)]
-    return [[device(z + half, y, x, c) for half in (1, 0) for y, x in chips] for z in range(0, 16, 2) for c in (0, 1)]
+    return [[device(z + half, y, x, part) for half in (1, 0) for y, x in chips] for z in range(0, 16, 2) for part in (0, 1)]
 
 
 def column_groups():
-    order = [(8 + n // 2 * 2 + 8 * (n % 2)) % 16 for n in range(8)]
-    rest = [(half, y, x, c) for half in (0, 1) for y in range(4) for x in range(4) for c in (0, 1)]
-    return [[device(z + half, y, x, c) for z in order] for half, y, x, c in rest]
+    order = range(8, 24, 2)
+    rest = [(half, y, x, part) for half in (0, 1) for y in range(4) for x in range(4) for part in (0, 1)]
+    return [[device(z + half, y, x, part) for z in order] for half, y, x, part in rest]
 
 
 def horner(coefs, u):
@@ -209,7 +210,7 @@
     out_ref[...] = jnp.broadcast_to(out[0:SHARD], out_ref.shape)
 
 
-def apply_kernel(atoms_ref, w_ref, energy_ref, force_ref, turned_ref):
+def apply_kernel(cross_ref, atoms_ref, w_ref, energy_ref, force_ref, turned_ref):
     x, y, z, charges = atoms_ref[8:9, :], atoms_ref[9:10, :], atoms_ref[10:11, :], atoms_ref[0:8, :]
     atoms = x.shape[1]
     cx, sx = table(x)
@@ -221,7 +222,8 @@
     ds = [-n * cq[n] for n in range(TOP + 1)]
     blank = [jnp.zeros((256 - HALF, atoms), F32)]
     high, low = split(jnp.concatenate([stack(cq, sq, blank), stack(dc, ds, blank)], axis=1))
-    w = stack([w_ref[core, n] for core in range(2) for tile in range(TILES) for n in (tile, TILES + tile)])
+    cross = cross_ref[0]
+    w = stack([w_ref[core, n] for core in (cross, 1 - cross) for tile in range(TILES) for n in (tile, TILES + tile)])
     w = jnp.concatenate([w[:, 0:256], pltpu.roll(w[:, 128:384], 256 - (HALF - 128), 1)], axis=0)
     w_high, w_low = split(w)
     turned_ref[...] = nn(jnp.concatenate([w_high, w_low, w_high], axis=1), jnp.concatenate([high, high, low], axis=0))
@@ -278,10 +280,11 @@
     atoms = positions.shape[1]
     copies = lax.axis_size("zh")
     shape = lambda *s: jax.ShapeDtypeStruct(s, F32)
-    core = lax.axis_index("c").astype(jnp.int32).reshape(1)
+    cross = lax.axis_index("zh").astype(jnp.int32).reshape(1)
+    part_of = lax.axis_index("c").astype(jnp.int32).reshape(1) ^ cross
     from_root = [(lax.axis_index(axis).astype(jnp.int32) + (4 - at)) % 4 for axis, at in zip(("y", "x"), ROOT)]
     tile = (from_root[0] * 4 + from_root[1]).reshape(1)
-    where = core * HALVES + tile * 2 + 1 - (lax.axis_index("zl").astype(jnp.int32) & 1)
+    where = part_of * HALVES + tile * 2 + 1 - (lax.axis_index("zl").astype(jnp.int32) & 1)
     rows = lambda a, first: jnp.pad(a, ((first, 16 - first - a.shape[0]), (0, 0)))
     own = rows(charges, 0) + rows(positions, 8) + rows(miller, 11).astype(F32)
     pair = lax.all_gather(own, "c")
@@ -296,7 +299,7 @@
     w = lax.all_to_all(w, AXES, 0, 0, axis_index_groups=layer, tiled=True)
     w = lax.all_gather(w, "c")
     wide = [pltpu.VMEM((4 * TILES * ROWS, 2 * atoms), F32)]
-    energy, force = call(apply_kernel, (shape(1, atoms), shape(3, atoms)), 2, wide)(own, w)
+    energy, force = call(apply_kernel, (shape(1, atoms), shape(3, atoms)), 2, wide, scalar=True)(cross, own, w)
     return energy.reshape(atoms), force
 
 

time: 55.8 us -> 54.6 us (0.978)
  blocking collectives: 51 us -> 49.8 us
    all_gather x1, blocking collectives: 5.21 us -> 2.08 us  [per_device(): w = lax.all_gather(w, 'c')]
    all_to_all x1, blocking collectives: 16.3 us -> 18.4 us  [per_device(): lax.all_to_all(part, AXES, 0, 0, axis_index_groups=column, tiled=True)]
where the time goes in v6:
time: 54.6 us; the launch traced here: 54.2 us
  blocking collectives  49.8 us (91%)
  Pallas kernels  2.99 us (5%)
  between operations  0.71 us (1%)
  local copies, waits for them, and re-layouts  0.69 us (1%)
    all_to_all x1, blocking collectives, per_device(): lax.all_to_all(part, AXES, 0, 0, axis_index_groups=column, tiled=True)  18.4 us
    all_to_all x1, blocking collectives, per_device(): w = lax.all_to_all(w, AXES, 0, 0, axis_index_groups=layer, tiled=True)  10.8 us
    all_to_all x1, blocking collectives, per_device(): part = lax.all_to_all(part, AXES, 0, 0, axis_index_groups=layer, tiled=True)  10.2 us
    all_gather x1, blocking collectives, per_device(): pair = lax.all_gather(own, 'c')  8.38 us
    all_gather x1, blocking collectives, per_device(): w = lax.all_gather(w, 'c')  2.08 us
    pallas_call x1, Pallas kernels, per_device(): call(apply_kernel, (shape(1, atoms), shape(3, atoms)), 2, wide, scalar=True)  1.8 us

profile of v6, /device:TPU:1, one launch (start us, length us, event | category | flops | bytes accessed | tf_op | source)
XLA Modules:
  0.0 54.2 jit_solution(3834815800360931311)
XLA Ops:
  0.6 0.0 copy-start
  0.7 0.0 copy-start.2
  0.7 0.0 copy-start.1
  0.7 0.7 %copy-done = f32[8,512]{1,0:T(8,128)S(1)} copy-done((f32[8,512]{1,0:T(8,128)S(1)}, f32[8,512]{1,0:T(8,128)}, u32[]{:S(2)}) %copy-start) | copy-done | bytes 16408
  1.4 0.0 copy-done.2
  1.4 0.0 copy-done.1
  1.4 8.4 %all-gather = f32[32,512]{1,0:T(8,128)S(1)} all-gather(f32[16,512]{1,0:T(8,128)S(1)} %convert_add_fusion.atoms_ref), channel_id=2, replica_groups=mesh['zl'=8,'y'=4,'zh'=2,'x'=4,'c'=2] {'c'}, dimensions={0}, use_global_device_ids=true | all-gather | bytes 98304 | tf_op jit(solution)/shard_map/all_gather | solution.py:290
  9.8 0.9 %shard_map.50 = f32[32,4,384]{2,1,0:T(4,128)S(1)} custom-call(s32[1]{0:T(128)S(6)} %sub.7.where_ref, f32[2,16,512]{2,1,0:T(8,128)S(1)} %bitcast.8), custom_call_target="tpu_custom_call" | custom-call | tf_op jit(solution)/shard_map/pallas_call | solution.py:293
  10.7 10.2 %all_to_all.15.part_ref = f32[32,4,384]{2,1,0:T(4,128)S(1)} all-to-all(f32[32,4,384]{2,1,0:T(4,128)S(1)} %shard_map.50), channel_id=1, replica_groups={{100,102,96,98,116,118,112,114,68,70,64,66,84,86,80,82,36,38,32,34,52,5..., dimensions={0} | all-to-all | bytes 393216 | tf_op jit(solution)/shard_map/all_to_all | solution.py:294
  20.9 0.1 shard_map.51
  21.0 18.4 %all_to_all.16.part_ref = f32[8,4,384]{2,1,0:T(4,128)S(1)} all-to-all(f32[8,4,384]{2,1,0:T(4,128)S(1)} %shard_map.51), channel_id=1, replica_groups={{9,137,265,393,0,128,256,384},{8,136,264,392,1,129,257,385},{11,139,267..., dimensions={0} | all-to-all | bytes 98304 | tf_op jit(solution)/shard_map/all_to_all | solution.py:296
  39.4 0.2 shard_map.52
  39.6 10.8 %all_to_all.17 = f32[32,4,384]{2,1,0:T(4,128)S(1)} all-to-all(f32[32,4,384]{2,1,0:T(4,128)S(1)} %shard_map.52), channel_id=1, replica_groups={{100,102,96,98,116,118,112,114,68,70,64,66,84,86,80,82,36,38,32,34,52,5..., dimensions={0} | all-to-all | bytes 393216 | tf_op jit(solution)/shard_map/all_to_all | solution.py:299
  50.4 2.1 %all-gather.1 = f32[64,4,384]{2,1,0:T(4,128)S(1)} all-gather(f32[32,4,384]{2,1,0:T(4,128)S(1)} %all_to_all.17), channel_id=3, replica_groups=mesh['zl'=8,'y'=4,'zh'=2,'x'=4,'c'=2] {'c'}, dimensions={0}, use_global_device_ids=true | all-gather | bytes 589824 | tf_op jit(solution)/shard_map/all_gather | solution.py:300
  52.4 1.8 %shard_map.53 = (f32[1,512]{1,0:T(1,128)}, f32[3,512]{1,0:T(4,128)}) custom-call(s32[1]{0:T(128)} %bitcast.cross_ref, f32[16,512]{1,0:T(8,128)S(1)} %convert_add_fusion.atoms_ref, f32[2,32,4,384]{3,2,1,0:T(4,128)S(1)} %bitcast.7), custom_call_target="tpu_custom_call" | custom-call | tf_op jit(solution)/shard_map/pallas_call | solution.py:302
  (1 shorter events, 0.0 us)
Async XLA Ops:
  0.6 0.7 %copy-start = (f32[8,512]{1,0:T(8,128)S(1)}, f32[8,512]{1,0:T(8,128)}, u32[]{:S(2)}) copy-start(f32[8,512]{1,0:T(8,128)} %param.4) | copy-start | bytes 49156
  0.7 0.7 %copy-start.2 = (f32[3,512]{1,0:T(4,128)S(1)}, f32[3,512]{1,0:T(4,128)}, u32[]{:S(2)}) copy-start(f32[3,512]{1,0:T(4,128)} %param.3) | copy-start | bytes 18436
  0.7 0.7 %copy-start.1 = (s32[3,512]{1,0:T(4,128)S(1)}, s32[3,512]{1,0:T(4,128)}, u32[]{:S(2)}) copy-start(s32[3,512]{1,0:T(4,128)} %param.5) | copy-start | bytes 18436

commit v7 on v6

--- a/solution.py
+++ b/solution.py
@@ -113,32 +113,35 @@
 
 def struct_kernel(where_ref, atoms_ref, out_ref, pairs_ref):
     core, mine = where_ref[0] // HALVES, where_ref[0] % HALVES // 2
-    both = jnp.concatenate([atoms_ref[0], atoms_ref[1]], axis=1)
-    lanes = both.shape[1]
-    x, z, charges = both[8:9], both[10:11], both[0:8]
-    y = both[9:10] * jnp.where(core == 0, 1.0, -1.0)
-    cx, sx = table(x)
-    cy, sy = table(y, steps=True)
-    cz, sz = table(z)
-
-    def keep(rows, value):
-        high, low = split(value)
-        pairs_ref[rows, 0:lanes] = high
-        pairs_ref[rows, lanes : 2 * lanes] = low
-        pairs_ref[rows, 2 * lanes : 3 * lanes] = high
-
-    for two in range(TILES // 2):
-        real, imag = [], []
-        for tile in (2 * two, 2 * two + 1):
-            cc, ss, sc, cs = factors(tile, cx, sx, cy, sy)
-            real.append(cc - ss)
-            imag.append(sc + cs)
-        keep(slice(16 * two, 16 * two + 16), stack(real))
-        keep(slice(128 + 16 * two, 128 + 16 * two + 16), stack(imag))
-    cq = z_rows(cz, charges)
-    sq = z_rows(sz, charges)
-    high, low = split(stack(cq, sq, [jnp.zeros((256 - HALF, lanes), F32)]))
-    sums = nt(pairs_ref[...], jnp.concatenate([high, high, low], axis=1))
+    sums = 0.0
+    for n in range(2):
+        own = atoms_ref[n]
+        lanes = own.shape[1]
+        first = 3 * lanes * n
+        x, z, charges = own[8:9], own[10:11], own[0:8]
+        y = own[9:10] * jnp.where(core == 0, 1.0, -1.0)
+        cx, sx = table(x)
+        cy, sy = table(y, steps=True)
+        cz, sz = table(z)
+
+        def keep(rows, value):
+            high, low = split(value)
+            pairs_ref[rows, first : first + lanes] = high
+            pairs_ref[rows, first + lanes : first + 2 * lanes] = low
+            pairs_ref[rows, first + 2 * lanes : first + 3 * lanes] = high
+
+        for two in range(TILES // 2):
+            real, imag = [], []
+            for tile in (2 * two, 2 * two + 1):
+                cc, ss, sc, cs = factors(tile, cx, sx, cy, sy)
+                real.append(cc - ss)
+                imag.append(sc + cs)
+            keep(slice(16 * two, 16 * two + 16), stack(real))
+            keep(slice(128 + 16 * two, 128 + 16 * two + 16), stack(imag))
+        cq = z_rows(cz, charges)
+        sq = z_rows(sz, charges)
+        high, low = split(stack(cq, sq, [jnp.zeros((256 - HALF, lanes), F32)]))
+        sums += nt(pairs_ref[:, first : first + 3 * lanes], jnp.concatenate([high, high, low], axis=1))
     real, imag = sums[0:128], pltpu.roll(sums[128:256], HALF - 128, 1)
     middle = real[:, 128:256] + imag[:, 0:128]
     for n in range(HALVES):
@@ -191,14 +194,14 @@
     a, b = jnp.where(tile == 15, 10, a), jnp.where(tile == 15, 10, b)
     square = jnp.maximum(a * a + b * b + c * c, 1).astype(F32)
     weight = jnp.exp(-0.025 * square) / square * scale
-    wide_lane = lax.broadcasted_iota(jnp.int32, (128, LANES), 1)
+    wide_lane = lax.broadcasted_iota(jnp.int32, (32, LANES), 1)
     wide_inner = jnp.where(wide_lane >= HALF, wide_lane - HALF, wide_lane)
     wide_c = jnp.where(wide_inner >= HALF // 2, wide_inner - HALF // 2, wide_inner) >> 3
-    offset = lax.broadcasted_iota(jnp.int32, (128, LANES), 0) - (TOP + COUNT_LANE - 256)
+    offset = lax.broadcasted_iota(jnp.int32, (32, LANES), 0) - TOP
     live = wide_lane < COUNT_LANE
     plus = (live & (offset == wide_c)).astype(F32)
     minus = (live & (offset == -wide_c) & (wide_c > 0)).astype(F32)
-    counts = total[:, 256:384].astype(BF16)
+    counts = pltpu.roll(total[:, 256:384], 32, 1)[:, 0:32].astype(BF16)
     both = nn(counts, (plus + minus).astype(BF16)) * (1.0 / copies)
     differ = nn(counts, (plus - minus).astype(BF16)) * (1.0 / copies)
     near, far = HALF // 2, HALF + HALF // 2

time: 54.6 us -> 54.6 us (level)
  no operation moved by 1% of the time
where the time goes in v7:
time: 54.6 us; the launch traced here: 54.2 us
  blocking collectives  49.8 us (91%)
  Pallas kernels  2.98 us (5%)
  between operations  0.71 us (1%)
  local copies, waits for them, and re-layouts  0.69 us (1%)
    all_to_all x1, blocking collectives, per_device(): lax.all_to_all(part, AXES, 0, 0, axis_index_groups=column, tiled=True)  18.4 us
    all_to_all x1, blocking collectives, per_device(): w = lax.all_to_all(w, AXES, 0, 0, axis_index_groups=layer, tiled=True)  10.8 us
    all_to_all x1, blocking collectives, per_device(): part = lax.all_to_all(part, AXES, 0, 0, axis_index_groups=layer, tiled=True)  10.2 us
    all_gather x1, blocking collectives, per_device(): pair = lax.all_gather(own, 'c')  8.38 us
    all_gather x1, blocking collectives, per_device(): w = lax.all_gather(w, 'c')  2.08 us
    pallas_call x1, Pallas kernels, per_device(): call(apply_kernel, (shape(1, atoms), shape(3, atoms)), 2, wide, scalar=True)  1.81 us

profile of v7, /device:TPU:1, one launch (start us, length us, event | category | flops | bytes accessed | tf_op | source)
XLA Modules:
  0.0 54.2 jit_solution(8070184987148272449)
XLA Ops:
  0.6 0.0 copy-start
  0.7 0.0 copy-start.2
  0.7 0.0 copy-start.1
  0.7 0.7 %copy-done = f32[8,512]{1,0:T(8,128)S(1)} copy-done((f32[8,512]{1,0:T(8,128)S(1)}, f32[8,512]{1,0:T(8,128)}, u32[]{:S(2)}) %copy-start) | copy-done | bytes 16408
  1.4 0.0 copy-done.2
  1.4 0.0 copy-done.1
  1.4 8.4 %all-gather = f32[32,512]{1,0:T(8,128)S(1)} all-gather(f32[16,512]{1,0:T(8,128)S(1)} %convert_add_fusion.atoms_ref), channel_id=2, replica_groups=mesh['zl'=8,'y'=4,'zh'=2,'x'=4,'c'=2] {'c'}, dimensions={0}, use_global_device_ids=true | all-gather | bytes 98304 | tf_op jit(solution)/shard_map/all_gather | solution.py:293
  9.8 0.9 %shard_map.50 = f32[32,4,384]{2,1,0:T(4,128)S(1)} custom-call(s32[1]{0:T(128)S(6)} %sub.7.where_ref, f32[2,16,512]{2,1,0:T(8,128)S(1)} %bitcast.8), custom_call_target="tpu_custom_call" | custom-call | tf_op jit(solution)/shard_map/pallas_call | solution.py:296
  10.7 10.2 %all_to_all.15.part_ref = f32[32,4,384]{2,1,0:T(4,128)S(1)} all-to-all(f32[32,4,384]{2,1,0:T(4,128)S(1)} %shard_map.50), channel_id=1, replica_groups={{100,102,96,98,116,118,112,114,68,70,64,66,84,86,80,82,36,38,32,34,52,5..., dimensions={0} | all-to-all | bytes 393216 | tf_op jit(solution)/shard_map/all_to_all | solution.py:297
  20.9 0.1 shard_map.51
  20.9 18.4 %all_to_all.16.part_ref = f32[8,4,384]{2,1,0:T(4,128)S(1)} all-to-all(f32[8,4,384]{2,1,0:T(4,128)S(1)} %shard_map.51), channel_id=1, replica_groups={{9,137,265,393,0,128,256,384},{8,136,264,392,1,129,257,385},{11,139,267..., dimensions={0} | all-to-all | bytes 98304 | tf_op jit(solution)/shard_map/all_to_all | solution.py:299
  39.3 0.2 shard_map.52
  39.6 10.8 %all_to_all.17 = f32[32,4,384]{2,1,0:T(4,128)S(1)} all-to-all(f32[32,4,384]{2,1,0:T(4,128)S(1)} %shard_map.52), channel_id=1, replica_groups={{100,102,96,98,116,118,112,114,68,70,64,66,84,86,80,82,36,38,32,34,52,5..., dimensions={0} | all-to-all | bytes 393216 | tf_op jit(solution)/shard_map/all_to_all | solution.py:302
  50.3 2.1 %all-gather.1 = f32[64,4,384]{2,1,0:T(4,128)S(1)} all-gather(f32[32,4,384]{2,1,0:T(4,128)S(1)} %all_to_all.17), channel_id=3, replica_groups=mesh['zl'=8,'y'=4,'zh'=2,'x'=4,'c'=2] {'c'}, dimensions={0}, use_global_device_ids=true | all-gather | bytes 589824 | tf_op jit(solution)/shard_map/all_gather | solution.py:303
  52.4 1.8 %shard_map.53 = (f32[1,512]{1,0:T(1,128)}, f32[3,512]{1,0:T(4,128)}) custom-call(s32[1]{0:T(128)} %bitcast.cross_ref, f32[16,512]{1,0:T(8,128)S(1)} %convert_add_fusion.atoms_ref, f32[2,32,4,384]{3,2,1,0:T(4,128)S(1)} %bitcast.7), custom_call_target="tpu_custom_call" | custom-call | tf_op jit(solution)/shard_map/pallas_call | solution.py:305
  (1 shorter events, 0.0 us)
Async XLA Ops:
  0.6 0.7 %copy-start = (f32[8,512]{1,0:T(8,128)S(1)}, f32[8,512]{1,0:T(8,128)}, u32[]{:S(2)}) copy-start(f32[8,512]{1,0:T(8,128)} %param.4) | copy-start | bytes 49156
  0.7 0.7 %copy-start.2 = (f32[3,512]{1,0:T(4,128)S(1)}, f32[3,512]{1,0:T(4,128)}, u32[]{:S(2)}) copy-start(f32[3,512]{1,0:T(4,128)} %param.3) | copy-start | bytes 18436
  0.7 0.7 %copy-start.1 = (s32[3,512]{1,0:T(4,128)S(1)}, s32[3,512]{1,0:T(4,128)}, u32[]{:S(2)}) copy-start(s32[3,512]{1,0:T(4,128)} %param.5) | copy-start | bytes 18436

commit v8 on v7

--- a/solution.py
+++ b/solution.py
@@ -35,7 +35,7 @@
 
 def device(z, y, x, part):
     z = z % 16
-    return int(np.arange(512).reshape(SHAPE)[z % 8, y, z // 8, x, part ^ (z // 8)])
+    return int(np.arange(512).reshape(SHAPE)[z % 8, y, z // 8, x, part ^ (1 - z // 8)])
 
 
 def layer_groups():
@@ -283,7 +283,7 @@
     atoms = positions.shape[1]
     copies = lax.axis_size("zh")
     shape = lambda *s: jax.ShapeDtypeStruct(s, F32)
-    cross = lax.axis_index("zh").astype(jnp.int32).reshape(1)
+    cross = 1 - lax.axis_index("zh").astype(jnp.int32).reshape(1)
     part_of = lax.axis_index("c").astype(jnp.int32).reshape(1) ^ cross
     from_root = [(lax.axis_index(axis).astype(jnp.int32) + (4 - at)) % 4 for axis, at in zip(("y", "x"), ROOT)]
     tile = (from_root[0] * 4 + from_root[1]).reshape(1)

time: 54.6 us -> 54.6 us (level)
  no operation moved by 1% of the time
where the time goes in v8:
time: 54.6 us; the launch traced here: 54.2 us
  blocking collectives  49.8 us (91%)
  Pallas kernels  2.97 us (5%)
  between operations  0.71 us (1%)
  local copies, waits for them, and re-layouts  0.69 us (1%)
    all_to_all x1, blocking collectives, per_device(): lax.all_to_all(part, AXES, 0, 0, axis_index_groups=column, tiled=True)  18.4 us
    all_to_all x1, blocking collectives, per_device(): w = lax.all_to_all(w, AXES, 0, 0, axis_index_groups=layer, tiled=True)  10.8 us
    all_to_all x1, blocking collectives, per_device(): part = lax.all_to_all(part, AXES, 0, 0, axis_index_groups=layer, tiled=True)  10.2 us
    all_gather x1, blocking collectives, per_device(): pair = lax.all_gather(own, 'c')  8.38 us
    all_gather x1, blocking collectives, per_device(): w = lax.all_gather(w, 'c')  2.08 us
    pallas_call x1, Pallas kernels, per_device(): call(apply_kernel, (shape(1, atoms), shape(3, atoms)), 2, wide, scalar=True)  1.8 us

profile of v8, /device:TPU:1, one launch (start us, length us, event | category | flops | bytes accessed | tf_op | source)
XLA Modules:
  0.0 54.2 jit_solution(8713283664980523820)
XLA Ops:
  0.6 0.0 copy-start
  0.7 0.0 copy-start.2
  0.7 0.0 copy-start.1
  0.7 0.7 %copy-done = f32[8,512]{1,0:T(8,128)S(1)} copy-done((f32[8,512]{1,0:T(8,128)S(1)}, f32[8,512]{1,0:T(8,128)}, u32[]{:S(2)}) %copy-start) | copy-done | bytes 16408
  1.4 0.0 copy-done.2
  1.4 0.0 copy-done.1
  1.4 8.4 %all-gather = f32[32,512]{1,0:T(8,128)S(1)} all-gather(f32[16,512]{1,0:T(8,128)S(1)} %convert_add_fusion.atoms_ref), channel_id=2, replica_groups=mesh['zl'=8,'y'=4,'zh'=2,'x'=4,'c'=2] {'c'}, dimensions={0}, use_global_device_ids=true | all-gather | bytes 98304 | tf_op jit(solution)/shard_map/all_gather | solution.py:293
  9.8 0.9 %shard_map.50 = f32[32,4,384]{2,1,0:T(4,128)S(1)} custom-call(s32[1]{0:T(128)S(6)} %sub.14.where_ref, f32[2,16,512]{2,1,0:T(8,128)S(1)} %bitcast.8), custom_call_target="tpu_custom_call" | custom-call | tf_op jit(solution)/shard_map/pallas_call | solution.py:296
  10.7 10.2 %all_to_all.15.part_ref = f32[32,4,384]{2,1,0:T(4,128)S(1)} all-to-all(f32[32,4,384]{2,1,0:T(4,128)S(1)} %shard_map.50), channel_id=1, replica_groups={{101,103,97,99,117,119,113,115,69,71,65,67,85,87,81,83,37,39,33,35,53,5..., dimensions={0} | all-to-all | bytes 393216 | tf_op jit(solution)/shard_map/all_to_all | solution.py:297
  20.9 0.1 shard_map.51
  20.9 18.4 %all_to_all.16.part_ref = f32[8,4,384]{2,1,0:T(4,128)S(1)} all-to-all(f32[8,4,384]{2,1,0:T(4,128)S(1)} %shard_map.51), channel_id=1, replica_groups={{8,136,264,392,1,129,257,385},{9,137,265,393,0,128,256,384},{10,138,266..., dimensions={0} | all-to-all | bytes 98304 | tf_op jit(solution)/shard_map/all_to_all | solution.py:299
  39.3 0.2 shard_map.52
  39.6 10.8 %all_to_all.17 = f32[32,4,384]{2,1,0:T(4,128)S(1)} all-to-all(f32[32,4,384]{2,1,0:T(4,128)S(1)} %shard_map.52), channel_id=1, replica_groups={{101,103,97,99,117,119,113,115,69,71,65,67,85,87,81,83,37,39,33,35,53,5..., dimensions={0} | all-to-all | bytes 393216 | tf_op jit(solution)/shard_map/all_to_all | solution.py:302
  50.3 2.1 %all-gather.1 = f32[64,4,384]{2,1,0:T(4,128)S(1)} all-gather(f32[32,4,384]{2,1,0:T(4,128)S(1)} %all_to_all.17), channel_id=3, replica_groups=mesh['zl'=8,'y'=4,'zh'=2,'x'=4,'c'=2] {'c'}, dimensions={0}, use_global_device_ids=true | all-gather | bytes 589824 | tf_op jit(solution)/shard_map/all_gather | solution.py:303
  52.4 1.8 %shard_map.53 = (f32[1,512]{1,0:T(1,128)}, f32[3,512]{1,0:T(4,128)}) custom-call(s32[1]{0:T(128)} %bitcast.cross_ref, f32[16,512]{1,0:T(8,128)S(1)} %convert_add_fusion.atoms_ref, f32[2,32,4,384]{3,2,1,0:T(4,128)S(1)} %bitcast.7), custom_call_target="tpu_custom_call" | custom-call | tf_op jit(solution)/shard_map/pallas_call | solution.py:305
  (1 shorter events, 0.0 us)
Async XLA Ops:
  0.6 0.7 %copy-start = (f32[8,512]{1,0:T(8,128)S(1)}, f32[8,512]{1,0:T(8,128)}, u32[]{:S(2)}) copy-start(f32[8,512]{1,0:T(8,128)} %param.4) | copy-start | bytes 49156
  0.7 0.7 %copy-start.2 = (f32[3,512]{1,0:T(4,128)S(1)}, f32[3,512]{1,0:T(4,128)}, u32[]{:S(2)}) copy-start(f32[3,512]{1,0:T(4,128)} %param.3) | copy-start | bytes 18436
  0.7 0.7 %copy-start.1 = (s32[3,512]{1,0:T(4,128)S(1)}, s32[3,512]{1,0:T(4,128)}, u32[]{:S(2)}) copy-start(s32[3,512]{1,0:T(4,128)} %param.5) | copy-start | bytes 18436

commit v9 on v8

--- a/solution.py
+++ b/solution.py
@@ -18,14 +18,7 @@
 LANES = 384
 COUNT_LANE = 352
 SIN = (3.141592640130706, -5.167710083507839, 2.550077523214083, -0.5982912856178239, 0.07765766030006041)
-COS = (
-    1.0,
-    -4.934802137078852,
-    4.058709159556494,
-    -1.3352120030499017,
-    0.23493731380758293,
-    -0.02439632432974524,
-)
+COS = (0.9999999532476084, -4.934792830619647, 4.058411352862679, -1.3318765680811553, 0.21968961109773877)
 F32 = jnp.float32
 BF16 = jnp.bfloat16
 SHAPE = (8, 4, 2, 4, 2)

time: 54.6 us -> 54.6 us (level)
  no operation moved by 1% of the time
where the time goes in v9:
time: 54.6 us; the launch traced here: 54.2 us
  blocking collectives  49.8 us (91%)
  Pallas kernels  2.94 us (5%)
  between operations  0.71 us (1%)
  local copies, waits for them, and re-layouts  0.69 us (1%)
    all_to_all x1, blocking collectives, per_device(): lax.all_to_all(part, AXES, 0, 0, axis_index_groups=column, tiled=True)  18.4 us
    all_to_all x1, blocking collectives, per_device(): w = lax.all_to_all(w, AXES, 0, 0, axis_index_groups=layer, tiled=True)  10.8 us
    all_to_all x1, blocking collectives, per_device(): part = lax.all_to_all(part, AXES, 0, 0, axis_index_groups=layer, tiled=True)  10.2 us
    all_gather x1, blocking collectives, per_device(): pair = lax.all_gather(own, 'c')  8.38 us
    all_gather x1, blocking collectives, per_device(): w = lax.all_gather(w, 'c')  2.08 us
    pallas_call x1, Pallas kernels, per_device(): call(apply_kernel, (shape(1, atoms), shape(3, atoms)), 2, wide, scalar=True)  1.79 us

profile of v9, /device:TPU:1, one launch (start us, length us, event | category | flops | bytes accessed | tf_op | source)
XLA Modules:
  0.0 54.2 jit_solution(10783532527386623460)
XLA Ops:
  0.6 0.0 copy-start
  0.7 0.0 copy-start.2
  0.7 0.0 copy-start.1
  0.7 0.7 %copy-done = f32[8,512]{1,0:T(8,128)S(1)} copy-done((f32[8,512]{1,0:T(8,128)S(1)}, f32[8,512]{1,0:T(8,128)}, u32[]{:S(2)}) %copy-start) | copy-done | bytes 16408
  1.4 0.0 copy-done.2
  1.4 0.0 copy-done.1
  1.4 8.4 %all-gather = f32[32,512]{1,0:T(8,128)S(1)} all-gather(f32[16,512]{1,0:T(8,128)S(1)} %convert_add_fusion.atoms_ref), channel_id=2, replica_groups=mesh['zl'=8,'y'=4,'zh'=2,'x'=4,'c'=2] {'c'}, dimensions={0}, use_global_device_ids=true | all-gather | bytes 98304 | tf_op jit(solution)/shard_map/all_gather | solution.py:286
  9.8 0.9 %shard_map.50 = f32[32,4,384]{2,1,0:T(4,128)S(1)} custom-call(s32[1]{0:T(128)S(6)} %sub.14.where_ref, f32[2,16,512]{2,1,0:T(8,128)S(1)} %bitcast.8), custom_call_target="tpu_custom_call" | custom-call | tf_op jit(solution)/shard_map/pallas_call | solution.py:289
  10.7 10.2 %all_to_all.15.part_ref = f32[32,4,384]{2,1,0:T(4,128)S(1)} all-to-all(f32[32,4,384]{2,1,0:T(4,128)S(1)} %shard_map.50), channel_id=1, replica_groups={{101,103,97,99,117,119,113,115,69,71,65,67,85,87,81,83,37,39,33,35,53,5..., dimensions={0} | all-to-all | bytes 393216 | tf_op jit(solution)/shard_map/all_to_all | solution.py:290
  20.9 0.1 shard_map.51
  20.9 18.4 %all_to_all.16.part_ref = f32[8,4,384]{2,1,0:T(4,128)S(1)} all-to-all(f32[8,4,384]{2,1,0:T(4,128)S(1)} %shard_map.51), channel_id=1, replica_groups={{8,136,264,392,1,129,257,385},{9,137,265,393,0,128,256,384},{10,138,266..., dimensions={0} | all-to-all | bytes 98304 | tf_op jit(solution)/shard_map/all_to_all | solution.py:292
  39.3 0.2 shard_map.52
  39.5 10.8 %all_to_all.17 = f32[32,4,384]{2,1,0:T(4,128)S(1)} all-to-all(f32[32,4,384]{2,1,0:T(4,128)S(1)} %shard_map.52), channel_id=1, replica_groups={{101,103,97,99,117,119,113,115,69,71,65,67,85,87,81,83,37,39,33,35,53,5..., dimensions={0} | all-to-all | bytes 393216 | tf_op jit(solution)/shard_map/all_to_all | solution.py:295
  50.3 2.1 %all-gather.1 = f32[64,4,384]{2,1,0:T(4,128)S(1)} all-gather(f32[32,4,384]{2,1,0:T(4,128)S(1)} %all_to_all.17), channel_id=3, replica_groups=mesh['zl'=8,'y'=4,'zh'=2,'x'=4,'c'=2] {'c'}, dimensions={0}, use_global_device_ids=true | all-gather | bytes 589824 | tf_op jit(solution)/shard_map/all_gather | solution.py:296
  52.4 1.8 %shard_map.53 = (f32[1,512]{1,0:T(1,128)}, f32[3,512]{1,0:T(4,128)}) custom-call(s32[1]{0:T(128)} %bitcast.cross_ref, f32[16,512]{1,0:T(8,128)S(1)} %convert_add_fusion.atoms_ref, f32[2,32,4,384]{3,2,1,0:T(4,128)S(1)} %bitcast.7), custom_call_target="tpu_custom_call" | custom-call | tf_op jit(solution)/shard_map/pallas_call | solution.py:298
  (1 shorter events, 0.0 us)
Async XLA Ops:
  0.6 0.7 %copy-start = (f32[8,512]{1,0:T(8,128)S(1)}, f32[8,512]{1,0:T(8,128)}, u32[]{:S(2)}) copy-start(f32[8,512]{1,0:T(8,128)} %param.4) | copy-start | bytes 49156
  0.7 0.7 %copy-start.2 = (f32[3,512]{1,0:T(4,128)S(1)}, f32[3,512]{1,0:T(4,128)}, u32[]{:S(2)}) copy-start(f32[3,512]{1,0:T(4,128)} %param.3) | copy-start | bytes 18436
  0.7 0.7 %copy-start.1 = (s32[3,512]{1,0:T(4,128)S(1)}, s32[3,512]{1,0:T(4,128)}, u32[]{:S(2)}) copy-start(s32[3,512]{1,0:T(4,128)} %param.5) | copy-start | bytes 18436
